TPU v7x, 768 devices: a whole 4x8x12 slice. The times are simulated.
768 devices in a mesh: gz: 192 (over x, y_hi, z, core), xy: 4 (over y_lo).
Axes of the slice: x: 4, y: 8 (y_hi: 2, y_lo: 4; y = y_hi * 4 + y_lo), z: 12, core: 2. Of those that a mesh axis runs over, the one named last changes fastest.
Arguments:
- coords: float32 [3, 384, 8, 128], P(None, 'gz', 'xy'), may hold values from 0 to 1
- species: int32 [384, 8, 128], P('gz', 'xy'), may hold values from 0 to 7
- centers: int32 [384, 8, 128], P('gz', 'xy'), may hold values from 0 to 127
- others: int32 [384, 8, 128], P('gz', 'xy'), may hold values from 0 to 1151
- live_count: int32 [384, 8], P('gz', 'xy'), may hold values from 42 to 128
- in_weight: float32 [24, 128], replicated, may hold values from -1.25 to 1.25
- env_weight: float32 [128, 32], replicated, may hold values from -0.5 to 0.5
- up_weight: float32 [160, 128], replicated, may hold values from -0.5 to 0.5
- out_weight: float32 [128], replicated, may hold values from -0.5 to 0.5
Outputs:
- atom_energy: float32 [384, 8, 128], P('gz', 'xy')
- forces: float32 [3, 384, 8, 128], P(None, 'gz', 'xy')
Inputs may be any that keep to these rules, and one draw needn't show every extreme that they name: Edge slots at or after live_count of a bin are padding; at most 128 are live.
All inputs are finite; a program needn't handle non-finite values.
Results may differ from a plain program's by a relative error of at most 0.0018.
Values may be sent and summed in bfloat16 or wider, within the bound.
No kernel may reach another device: no remote copies, remote signals or barrier semaphores. Data moves between devices by JAX's collectives and lax.ppermute only.
A program may use at most 32 MiB of HBM per device.

v0:
```python
import jax
import jax.numpy as jnp
from jax import lax
from jax.sharding import PartitionSpec as P

NB = 8
SPEC = 8


SOFTEN = 0.01
CUTOFF = 3.5
HIGH = lax.Precision.HIGHEST


def extended_2(block, sides, width):
    for axis, dim in sides:
        count = lax.axis_size(axis)
        forward = [(i, i + 1) for i in range(count - 1)]
        forward.append((count - 1, 0))
        backward = [(target, source) for source, target in forward]
        low = lax.ppermute(
            lax.slice_in_dim(block, block.shape[dim] - width, None, axis=dim), axis, forward
        )
        high = lax.ppermute(lax.slice_in_dim(block, 0, width, axis=dim), axis, backward)
        block = jnp.concatenate([low, block, high], axis=dim)
    return block


def atom_table(indices):
    return (indices[..., None] == jnp.arange(128)).astype(jnp.float32)


def pick_center(lattice, center_hot):
    return jnp.einsum("fabn,aben->fabe", lattice, center_hot, precision=HIGH)


def pick_other(lattice_ext, others):
    depth_bins = lattice_ext.shape[-3] - 2
    span_bins = lattice_ext.shape[-2] - 2
    other_hot = atom_table(others % 128)
    placement = others // 128
    gathered = jnp.zeros((lattice_ext.shape[0],) + others.shape, jnp.float32)
    for offset in range(9):
        start_z = offset // 3
        start_x = offset % 3
        block = lattice_ext[:, start_z : start_z + depth_bins, start_x : start_x + span_bins, :]
        chosen = (placement == offset).astype(jnp.float32)[None]
        gathered = (
            gathered + jnp.einsum("fabn,aben->fabe", block, other_hot, precision=HIGH) * chosen
        )
    return gathered


def live_mask(live_count, edge_count):
    return (jnp.arange(edge_count)[None, None, :] < live_count[..., None]).astype(jnp.float32)


def geometry(coord_ext, spec_ext, centers, others, in_weight):
    center_hot = atom_table(centers)
    at_center = pick_center(coord_ext[:, 1:-1, 1:-1], center_hot)
    at_other = pick_other(coord_ext, others)
    placement = others // 128
    shift_z = (placement // 3 - 1).astype(jnp.float32)
    shift_x = (placement % 3 - 1).astype(jnp.float32)
    along_z = shift_z + at_other[0] - at_center[0]
    across = shift_x + at_other[1] - at_center[1]
    along_y = at_other[2] - at_center[2]
    distance = jnp.sqrt(along_z * along_z + across * across + along_y * along_y + SOFTEN)
    scaled = distance / CUTOFF
    envelope = (1.0 - scaled * scaled) ** 2
    orders = jnp.arange(1, NB + 1).astype(jnp.float32)[:, None, None, None]
    radial = jnp.sin(orders * jnp.pi * scaled[None]) / distance[None] * envelope[None]
    species_ids = jnp.arange(SPEC)[:, None, None, None]
    spec_table = (spec_ext[None] == species_ids).astype(jnp.float32)
    spec_center = pick_center(spec_table[:, 1:-1, 1:-1], center_hot)
    spec_other = pick_other(spec_table, others)
    inputs = jnp.concatenate([radial, spec_center, spec_other], axis=0)
    latent = jax.nn.silu(jnp.einsum("kabe,kl->labe", inputs, in_weight, precision=HIGH))
    harmonics = jnp.stack(
        [jnp.ones_like(distance), along_z / distance, across / distance, along_y / distance]
    )
    return (latent, harmonics, envelope)


def features(latent, harmonics, centers, live_count, env_weight):
    edge_count = centers.shape[-1]
    weights = (
        jnp.einsum("labe,lc->cabe", latent, env_weight, precision=HIGH)
        * live_mask(live_count, edge_count)[None]
    )
    messages = (weights[:, None] * harmonics[None]).reshape((-1,) + centers.shape)
    one_hot = atom_table(centers)
    return jnp.einsum("fabe,aben->fabn", messages, one_hot, precision=HIGH) * (128.0 / edge_count)


def energy(latent, envelope, feature_ext, centers, others, live_count, up_weight, out_weight):
    channels = feature_ext.shape[0] // 4
    one_hot = atom_table(centers)
    feat_center = pick_center(feature_ext[:, 1:-1, 1:-1], one_hot)
    feat_other = pick_other(feature_ext, others)
    products = (feat_center * feat_other).reshape((channels, 4) + centers.shape).sum(axis=1)
    joined = jnp.concatenate([latent, products], axis=0)
    hidden = jax.nn.silu(jnp.einsum("kabe,kl->labe", joined, up_weight, precision=HIGH))
    edge_energy = (
        jnp.einsum("labe,l->abe", hidden, out_weight, precision=HIGH)
        * envelope
        * live_mask(live_count, centers.shape[-1])
    )
    atom_energy = jnp.einsum("abe,aben->abn", edge_energy, one_hot, precision=HIGH)
    return (jnp.sum(edge_energy), atom_energy)


def fold_wide(ghost, depth):
    padded = extended_2(ghost, (("gz", 1), ("xy", 2)), depth)
    rows_z = ghost.shape[1] - 2 * depth
    rows_x = ghost.shape[2] - 2 * depth
    parts_z = [
        (slice(0, depth), slice(0, depth)),
        (slice(2 * depth, 2 * depth + rows_z), slice(0, rows_z)),
        (slice(rows_z + 3 * depth, rows_z + 4 * depth), slice(rows_z - depth, rows_z)),
    ]
    parts_x = [
        (slice(0, depth), slice(0, depth)),
        (slice(2 * depth, 2 * depth + rows_x), slice(0, rows_x)),
        (slice(rows_x + 3 * depth, rows_x + 4 * depth), slice(rows_x - depth, rows_x)),
    ]
    result = jnp.zeros((ghost.shape[0], rows_z, rows_x, ghost.shape[3]), jnp.float32)
    for source_z, target_z in parts_z:
        for source_x, target_x in parts_x:
            result = result.at[:, target_z, target_x].add(padded[:, source_z, source_x])
    return result


def body(
    coords, species, centers, others, live_count, in_weight, env_weight, up_weight, out_weight
):
    packed = jnp.concatenate([coords, species.astype(jnp.float32)[None]], axis=0)
    extended = extended_2(packed, (("gz", 1), ("xy", 2)), 2)
    spec_wide = extended[3].astype(jnp.int32)
    coord_wide = extended[:3]
    edge_count = centers.shape[-1]
    lists = jnp.concatenate([centers, others, live_count[..., None]], axis=-1)
    lists_ext = extended_2(lists, (("gz", 0), ("xy", 1)), 1)
    centers_ext = lists_ext[..., :edge_count]
    others_ext = lists_ext[..., edge_count : 2 * edge_count]
    live_ext = lists_ext[..., 2 * edge_count]

    def whole_energy(coord_now):
        latent, harmonics, envelope = geometry(
            coord_now, spec_wide, centers_ext, others_ext, in_weight
        )
        feat = features(latent, harmonics, centers_ext, live_ext, env_weight)
        rounded = lax.optimization_barrier(feat.astype(jnp.bfloat16)).astype(jnp.float32)
        through = feat + lax.stop_gradient(rounded - feat)
        return energy(
            latent[:, 1:-1, 1:-1],
            envelope[1:-1, 1:-1],
            through,
            centers,
            others,
            live_count,
            up_weight,
            out_weight,
        )

    (energy_sum, atom_energy), coord_grad = jax.value_and_grad(whole_energy, has_aux=True)(
        coord_wide
    )
    forces = -fold_wide(coord_grad, 2)
    return (atom_energy, forces)


def solution(mesh):
    in_specs = (
        P(None, "gz", "xy", None),
        P("gz", "xy", None),
        P("gz", "xy", None),
        P("gz", "xy", None),
        P("gz", "xy"),
        P(),
        P(),
        P(),
        P(),
    )
    out_specs = (P("gz", "xy", None), P(None, "gz", "xy", None))
    return jax.shard_map(body, mesh=mesh, in_specs=in_specs, out_specs=out_specs, check_vma=False)
```

profile of v0, /device:TPU:24, one launch (start us, length us, event | category | flops | bytes accessed | tf_op | source)
XLA Modules:
  0.0 135.5 jit_solution(6659626452617429492)
XLA Ops:
  2.1 18.8 %collective-permute-start.5 = (f32[4,2,2,128]{3,0,2,1:T(4,128)S(1)}, f32[4,2,2,128]{3,0,2,1:T(4,128)S(1)}, u32[]{:S(2)}, u32[]{:S(2)}) collective-permute-start(f32[4,2,2,128]{3,0,2,1:T(4,128)S(1)} %pad_maximum_fusion.7), channel_id=1, source_target_pairs={{4,0},{8,4},{12,8},{16,12},{20,16},{24,20},{28,24},{32,28},{36,32}... | collective-permute-start | bytes 24584 | tf_op jit(solution)/shard_map/ppermute | solution.py:24
  20.9 1.9 %collective-permute-start.4 = (f32[4,2,2,128]{3,0,2,1:T(4,128)S(1)}, f32[4,2,2,128]{3,0,2,1:T(4,128)S(1)}, u32[]{:S(2)}, u32[]{:S(2)}) collective-permute-start(f32[4,2,2,128]{3,0,2,1:T(4,128)S(1)} %pad_maximum_fusion.7), channel_id=1, source_target_pairs={{0,4},{4,8},{8,12},{12,16},{16,20},{20,24},{24,28},{28,32},{32,36}... | collective-permute-start | bytes 24584 | tf_op jit(solution)/shard_map/ppermute | solution.py:21
  22.9 1.9 %collective-permute-start = (s32[1,2,257]{2,1,0:T(2,128)S(1)}, s32[1,2,257]{2,1,0:T(2,128)S(1)}, u32[]{:S(2)}, u32[]{:S(2)}) collective-permute-start(s32[1,2,257]{2,1,0:T(2,128)S(1)} %get-tuple-element.249), channel_id=1, source_target_pairs={{0,4},{4,8},{8,12},{12,16},{16,20},{20,24},{24,28},{28,32},{32,36}... | collective-permute-start | bytes 6176 | tf_op jit(solution)/shard_map/ppermute | solution.py:21
  24.9 11.8 %collective-permute-start.1 = (s32[1,2,257]{2,1,0:T(2,128)S(1)}, s32[1,2,257]{2,1,0:T(2,128)S(1)}, u32[]{:S(2)}, u32[]{:S(2)}) collective-permute-start(s32[1,2,257]{2,1,0:T(2,128)S(1)} %get-tuple-element.250), channel_id=1, source_target_pairs={{4,0},{8,4},{12,8},{16,12},{20,16},{24,20},{28,24},{32,28},{36,32}... | collective-permute-start | bytes 6176 | tf_op jit(solution)/shard_map/ppermute | solution.py:24
  36.7 1.2 collective-permute-done.1
  38.0 4.8 %collective-permute-start.2 = (s32[4,1,257]{2,1,0:T(1,128)S(1)}, s32[4,1,257]{2,1,0:T(1,128)S(1)}, u32[]{:S(2)}, u32[]{:S(2)}) collective-permute-start(s32[4,1,257]{2,1,0:T(1,128)S(1)} %get-tuple-element.232), channel_id=1, source_target_pairs={{0,1},{1,2},{2,3},{3,0},{4,5},{5,6},{6,7},{7,4},{8,9},{9,10},{10,1... | collective-permute-start | bytes 12344 | tf_op jit(solution)/shard_map/ppermute | solution.py:21
  42.8 1.9 %collective-permute-start.3 = (s32[4,1,257]{2,1,0:T(1,128)S(1)}, s32[4,1,257]{2,1,0:T(1,128)S(1)}, u32[]{:S(2)}, u32[]{:S(2)}) collective-permute-start(s32[4,1,257]{2,1,0:T(1,128)S(1)} %get-tuple-element.233), channel_id=1, source_target_pairs={{1,0},{2,1},{3,2},{0,3},{5,4},{6,5},{7,6},{4,7},{9,8},{10,9},{11,1... | collective-permute-start | bytes 12344 | tf_op jit(solution)/shard_map/ppermute | solution.py:24
  44.8 5.4 %collective-permute-done.3 = s32[4,1,257]{2,1,0:T(1,128)S(1)} collective-permute-done((s32[4,1,257]{2,1,0:T(1,128)S(1)}, s32[4,1,257]{2,1,0:T(1,128)S(1)}, u32[]{:S(2)}, u32[]{:S(2)}) %collective-permute-start.3) | collective-permute-done | bytes 4144 | tf_op jit(solution)/shard_map/ppermute | solution.py:24
  50.4 1.9 %collective-permute-start.7 = (f32[4,6,2,128]{3,0,2,1:T(4,128)S(1)}, f32[4,6,2,128]{3,0,2,1:T(4,128)S(1)}, u32[]{:S(2)}, u32[]{:S(2)}) collective-permute-start(f32[4,6,2,128]{3,0,2,1:T(4,128)S(1)} %pad_maximum_fusion.6), channel_id=1, source_target_pairs={{1,0},{2,1},{3,2},{0,3},{5,4},{6,5},{7,6},{4,7},{9,8},{10,9},{11,1... | collective-permute-start | bytes 73736 | tf_op jit(solution)/shard_map/ppermute | solution.py:24
  52.3 5.7 %collective-permute-start.6 = (f32[4,6,2,128]{3,0,2,1:T(4,128)S(1)}, f32[4,6,2,128]{3,0,2,1:T(4,128)S(1)}, u32[]{:S(2)}, u32[]{:S(2)}) collective-permute-start(f32[4,6,2,128]{3,0,2,1:T(4,128)S(1)} %pad_maximum_fusion.6), channel_id=1, source_target_pairs={{0,1},{1,2},{2,3},{3,0},{4,5},{5,6},{6,7},{7,4},{8,9},{9,10},{10,1... | collective-permute-start | bytes 73736 | tf_op jit(solution)/shard_map/ppermute | solution.py:21
  58.1 1.4 %collective-permute-done.6 = f32[4,6,2,128]{3,0,2,1:T(4,128)S(1)} collective-permute-done((f32[4,6,2,128]{3,0,2,1:T(4,128)S(1)}, f32[4,6,2,128]{3,0,2,1:T(4,128)S(1)}, u32[]{:S(2)}, u32[]{:S(2)}) %collective-permute-start.6) | collective-permute-done | bytes 24608 | tf_op jit(solution)/shard_map/ppermute | solution.py:21
  65.3 1.0 fusion.27
  76.8 1.2 fusion.55
  79.7 2.0 %fusion.244 = (bf16[128,4,4,128]{0,3,2,1:T(8,128)(2,1)S(1)}, f32[128,4,4,128]{0,3,2,1:T(8,128)S(1)}) fusion(f32[128,4,4,128]{3,0,2,1:T(8,128)S(1)} %bitcast.240, s32[4,4,128]{2,1,0:T(4,128)S(1)} %get-tuple-element.231), kind=kOutput, calls=%fused_computation.413 | convolution fusion | flops 403439616 | bytes 2629632 | tf_op jit(solution)/shard_map/jvp(fabe,aben->fabn)/dot_general | solution.py:93
  86.8 1.1 convolution_bitcast_fusion.4
  93.5 1.3 fusion.32
  95.8 1.0 fusion
  96.8 1.2 convolution_bitcast_fusion.16
  105.9 1.9 %collective-permute-start.8 = (f32[3,2,6,128]{3,0,2,1:T(4,128)S(1)}, f32[3,2,6,128]{3,0,2,1:T(4,128)S(1)}, u32[]{:S(2)}, u32[]{:S(2)}) collective-permute-start(f32[3,2,6,128]{3,0,2,1:T(4,128)S(1)} %get-tuple-element.211), channel_id=1, source_target_pairs={{0,4},{4,8},{8,12},{12,16},{16,20},{20,24},{24,28},{28,32},{32,36}... | collective-permute-start | bytes 55304 | tf_op jit(solution)/shard_map/ppermute | solution.py:21
  107.8 11.8 %collective-permute-start.9 = (f32[3,2,6,128]{3,0,2,1:T(4,128)S(1)}, f32[3,2,6,128]{3,0,2,1:T(4,128)S(1)}, u32[]{:S(2)}, u32[]{:S(2)}) collective-permute-start(f32[3,2,6,128]{3,0,2,1:T(4,128)S(1)} %get-tuple-element.212), channel_id=1, source_target_pairs={{4,0},{8,4},{12,8},{16,12},{20,16},{24,20},{28,24},{32,28},{36,32}... | collective-permute-start | bytes 55304 | tf_op jit(solution)/shard_map/ppermute | solution.py:24
  119.6 1.5 %collective-permute-done.9 = f32[3,2,6,128]{3,0,2,1:T(4,128)S(1)} collective-permute-done((f32[3,2,6,128]{3,0,2,1:T(4,128)S(1)}, f32[3,2,6,128]{3,0,2,1:T(4,128)S(1)}, u32[]{:S(2)}, u32[]{:S(2)}) %collective-permute-start.9) | collective-permute-done | bytes 18464 | tf_op jit(solution)/shard_map/ppermute | solution.py:24
  121.1 6.0 %collective-permute-start.10 = (f32[3,10,2,128]{3,0,2,1:T(4,128)S(1)}, f32[3,10,2,128]{3,0,2,1:T(4,128)S(1)}, u32[]{:S(2)}, u32[]{:S(2)}) collective-permute-start(f32[3,10,2,128]{3,0,2,1:T(4,128)S(1)} %get-tuple-element.209), channel_id=1, source_target_pairs={{0,1},{1,2},{2,3},{3,0},{4,5},{5,6},{6,7},{7,4},{8,9},{9,10},{10,1... | collective-permute-start | bytes 92168 | tf_op jit(solution)/shard_map/ppermute | solution.py:21
  127.2 1.9 %collective-permute-start.11 = (f32[3,10,2,128]{3,0,2,1:T(4,128)S(1)}, f32[3,10,2,128]{3,0,2,1:T(4,128)S(1)}, u32[]{:S(2)}, u32[]{:S(2)}) collective-permute-start(f32[3,10,2,128]{3,0,2,1:T(4,128)S(1)} %get-tuple-element.210), channel_id=1, source_target_pairs={{1,0},{2,1},{3,2},{0,3},{5,4},{6,5},{7,6},{4,7},{9,8},{10,9},{11,1... | collective-permute-start | bytes 92168 | tf_op jit(solution)/shard_map/ppermute | solution.py:24
  130.0 4.9 %collective-permute-done.11 = f32[3,10,2,128]{3,0,2,1:T(4,128)S(1)} collective-permute-done((f32[3,10,2,128]{3,0,2,1:T(4,128)S(1)}, f32[3,10,2,128]{3,0,2,1:T(4,128)S(1)}, u32[]{:S(2)}, u32[]{:S(2)}) %collective-permute-start.11) | collective-permute-done | bytes 30752 | tf_op jit(solution)/shard_map/ppermute | solution.py:24
  (133 shorter events, 40.5 us)
Async XLA Ops:
  0.6 86.1 %copy-start = (f32[160,128]{1,0:T(8,128)S(1)}, f32[160,128]{1,0:T(8,128)}, u32[]{:S(2)}) copy-start(f32[160,128]{1,0:T(8,128)} %param.52) | copy-start | bytes 245764
  2.1 20.8 %copy-start.5 = (s32[2,2]{1,0:T(2,128)S(1)}, s32[2,2]{1,0:T(2,128)}, u32[]{:S(2)}) copy-start(s32[2,2]{1,0:T(2,128)} %param.49) | copy-start | bytes 52
  2.1 20.9 %copy-start.3 = (s32[2,2,128]{2,1,0:T(2,128)S(1)}, s32[2,2,128]{2,1,0:T(2,128)}, u32[]{:S(2)}) copy-start(s32[2,2,128]{2,1,0:T(2,128)} %param.47) | copy-start | bytes 6148
  2.1 20.8 %copy-start.4 = (s32[2,2,128]{2,1,0:T(2,128)S(1)}, s32[2,2,128]{2,1,0:T(2,128)}, u32[]{:S(2)}) copy-start(s32[2,2,128]{2,1,0:T(2,128)} %param.48) | copy-start | bytes 6148
  2.1 48.3 %collective-permute-start.5 = (f32[4,2,2,128]{3,0,2,1:T(4,128)S(1)}, f32[4,2,2,128]{3,0,2,1:T(4,128)S(1)}, u32[]{:S(2)}, u32[]{:S(2)}) collective-permute-start(f32[4,2,2,128]{3,0,2,1:T(4,128)S(1)} %pad_maximum_fusion.7), channel_id=1, source_target_pairs={{4,0},{8,4},{12,8},{16,12},{20,16},{24,20},{28,24},{32,28},{36,32}... | collective-permute-start | bytes 24584 | tf_op jit(solution)/shard_map/ppermute | solution.py:24
  20.9 29.5 %collective-permute-start.4 = (f32[4,2,2,128]{3,0,2,1:T(4,128)S(1)}, f32[4,2,2,128]{3,0,2,1:T(4,128)S(1)}, u32[]{:S(2)}, u32[]{:S(2)}) collective-permute-start(f32[4,2,2,128]{3,0,2,1:T(4,128)S(1)} %pad_maximum_fusion.7), channel_id=1, source_target_pairs={{0,4},{4,8},{8,12},{12,16},{16,20},{20,24},{24,28},{28,32},{32,36}... | collective-permute-start | bytes 24584 | tf_op jit(solution)/shard_map/ppermute | solution.py:21
  22.9 13.8 %collective-permute-start = (s32[1,2,257]{2,1,0:T(2,128)S(1)}, s32[1,2,257]{2,1,0:T(2,128)S(1)}, u32[]{:S(2)}, u32[]{:S(2)}) collective-permute-start(s32[1,2,257]{2,1,0:T(2,128)S(1)} %get-tuple-element.249), channel_id=1, source_target_pairs={{0,4},{4,8},{8,12},{12,16},{16,20},{20,24},{24,28},{28,32},{32,36}... | collective-permute-start | bytes 6176 | tf_op jit(solution)/shard_map/ppermute | solution.py:21
  24.9 13.1 %collective-permute-start.1 = (s32[1,2,257]{2,1,0:T(2,128)S(1)}, s32[1,2,257]{2,1,0:T(2,128)S(1)}, u32[]{:S(2)}, u32[]{:S(2)}) collective-permute-start(s32[1,2,257]{2,1,0:T(2,128)S(1)} %get-tuple-element.250), channel_id=1, source_target_pairs={{4,0},{8,4},{12,8},{16,12},{20,16},{24,20},{28,24},{32,28},{36,32}... | collective-permute-start | bytes 6176 | tf_op jit(solution)/shard_map/ppermute | solution.py:24
  38.0 6.8 %collective-permute-start.2 = (s32[4,1,257]{2,1,0:T(1,128)S(1)}, s32[4,1,257]{2,1,0:T(1,128)S(1)}, u32[]{:S(2)}, u32[]{:S(2)}) collective-permute-start(s32[4,1,257]{2,1,0:T(1,128)S(1)} %get-tuple-element.232), channel_id=1, source_target_pairs={{0,1},{1,2},{2,3},{3,0},{4,5},{5,6},{6,7},{7,4},{8,9},{9,10},{10,1... | collective-permute-start | bytes 12344 | tf_op jit(solution)/shard_map/ppermute | solution.py:21
  42.8 7.3 %collective-permute-start.3 = (s32[4,1,257]{2,1,0:T(1,128)S(1)}, s32[4,1,257]{2,1,0:T(1,128)S(1)}, u32[]{:S(2)}, u32[]{:S(2)}) collective-permute-start(s32[4,1,257]{2,1,0:T(1,128)S(1)} %get-tuple-element.233), channel_id=1, source_target_pairs={{1,0},{2,1},{3,2},{0,3},{5,4},{6,5},{7,6},{4,7},{9,8},{10,9},{11,1... | collective-permute-start | bytes 12344 | tf_op jit(solution)/shard_map/ppermute | solution.py:24
  50.4 7.7 %collective-permute-start.7 = (f32[4,6,2,128]{3,0,2,1:T(4,128)S(1)}, f32[4,6,2,128]{3,0,2,1:T(4,128)S(1)}, u32[]{:S(2)}, u32[]{:S(2)}) collective-permute-start(f32[4,6,2,128]{3,0,2,1:T(4,128)S(1)} %pad_maximum_fusion.6), channel_id=1, source_target_pairs={{1,0},{2,1},{3,2},{0,3},{5,4},{6,5},{7,6},{4,7},{9,8},{10,9},{11,1... | collective-permute-start | bytes 73736 | tf_op jit(solution)/shard_map/ppermute | solution.py:24
  52.3 7.2 %collective-permute-start.6 = (f32[4,6,2,128]{3,0,2,1:T(4,128)S(1)}, f32[4,6,2,128]{3,0,2,1:T(4,128)S(1)}, u32[]{:S(2)}, u32[]{:S(2)}) collective-permute-start(f32[4,6,2,128]{3,0,2,1:T(4,128)S(1)} %pad_maximum_fusion.6), channel_id=1, source_target_pairs={{0,1},{1,2},{2,3},{3,0},{4,5},{5,6},{6,7},{7,4},{8,9},{9,10},{10,1... | collective-permute-start | bytes 73736 | tf_op jit(solution)/shard_map/ppermute | solution.py:21
  76.1 0.7 copy-start.6
  78.0 0.7 copy-start.2
  86.8 1.1 copy-start.7
  88.9 0.7 copy-start.1
  94.8 1.0 slice-start
  105.9 13.7 %collective-permute-start.8 = (f32[3,2,6,128]{3,0,2,1:T(4,128)S(1)}, f32[3,2,6,128]{3,0,2,1:T(4,128)S(1)}, u32[]{:S(2)}, u32[]{:S(2)}) collective-permute-start(f32[3,2,6,128]{3,0,2,1:T(4,128)S(1)} %get-tuple-element.211), channel_id=1, source_target_pairs={{0,4},{4,8},{8,12},{12,16},{16,20},{20,24},{24,28},{28,32},{32,36}... | collective-permute-start | bytes 55304 | tf_op jit(solution)/shard_map/ppermute | solution.py:21
  107.8 13.3 %collective-permute-start.9 = (f32[3,2,6,128]{3,0,2,1:T(4,128)S(1)}, f32[3,2,6,128]{3,0,2,1:T(4,128)S(1)}, u32[]{:S(2)}, u32[]{:S(2)}) collective-permute-start(f32[3,2,6,128]{3,0,2,1:T(4,128)S(1)} %get-tuple-element.212), channel_id=1, source_target_pairs={{4,0},{8,4},{12,8},{16,12},{20,16},{24,20},{28,24},{32,28},{36,32}... | collective-permute-start | bytes 55304 | tf_op jit(solution)/shard_map/ppermute | solution.py:24
  121.1 8.9 %collective-permute-start.10 = (f32[3,10,2,128]{3,0,2,1:T(4,128)S(1)}, f32[3,10,2,128]{3,0,2,1:T(4,128)S(1)}, u32[]{:S(2)}, u32[]{:S(2)}) collective-permute-start(f32[3,10,2,128]{3,0,2,1:T(4,128)S(1)} %get-tuple-element.209), channel_id=1, source_target_pairs={{0,1},{1,2},{2,3},{3,0},{4,5},{5,6},{6,7},{7,4},{8,9},{9,10},{10,1... | collective-permute-start | bytes 92168 | tf_op jit(solution)/shard_map/ppermute | solution.py:21
  127.2 7.7 %collective-permute-start.11 = (f32[3,10,2,128]{3,0,2,1:T(4,128)S(1)}, f32[3,10,2,128]{3,0,2,1:T(4,128)S(1)}, u32[]{:S(2)}, u32[]{:S(2)}) collective-permute-start(f32[3,10,2,128]{3,0,2,1:T(4,128)S(1)} %get-tuple-element.210), channel_id=1, source_target_pairs={{1,0},{2,1},{3,2},{0,3},{5,4},{6,5},{7,6},{4,7},{9,8},{10,9},{11,1... | collective-permute-start | bytes 92168 | tf_op jit(solution)/shard_map/ppermute | solution.py:24
where the time goes:
time: 136 us; the launch traced here: 135 us
  starting transfers between devices  70.4 us (52%)
  matrix products  42.6 us (31%)
  waiting for transfers between devices  14.4 us (11%)
  other arithmetic  3.56 us (3%)
  local copies, waits for them, and re-layouts  3.2 us (2%)
  between operations  1.37 us (1%)
    ppermute x6, starting transfers between devices, extended_2(): lax.ppermute(lax.slice_in_dim(block, 0, width, axis=dim), axis, backward)  48.1 us
    dot_general x45, matrix products, pick_other(): jnp.einsum('fabn,aben->fabe', block, other_hot, precision=HIGH) * chosen  29 us
    ppermute x6, starting transfers between devices, extended_2(): lax.ppermute(lax.slice_in_dim(block, block.shape[dim] - width, None, axis...  22.3 us
    ppermute x6, waiting for transfers between devices, extended_2(): lax.ppermute(lax.slice_in_dim(block, 0, width, axis=dim), axis, backward)  12.9 us
    dot_general x2, matrix products, features(): jnp.einsum('fabe,aben->fabn', messages, one_hot, precision=HIGH)  3.27 us
    dot_general x5, matrix products, pick_center(): return jnp.einsum('fabn,aben->fabe', lattice, center_hot, precision=HIGH)  3.19 us
    unnamed x19, local copies, waits for them, and re-layouts  2.76 us
  transfers between devices with their start and end apart: 12, of which 5 were waited for; matrix products, arithmetic and copies ran while one was open for 1% of the time, Pallas kernels for 0%

commit v1 on v0

v1 whole, which is shorter than its diff:
```python
import jax
import jax.numpy as jnp
from jax import lax
from jax.experimental import pallas as pl
from jax.experimental.pallas import tpu as pltpu
from jax.sharding import PartitionSpec as P

NB = 8
SPEC = 8
LAT = 128
CH = 32
SOFTEN = 0.01
CUTOFF = 3.5
COLS = 8
F32 = jnp.float32
BF16 = jnp.bfloat16
PI = 3.141592653589793


def halves(value):
    high = value.astype(BF16)
    low = (value - high.astype(F32)).astype(BF16)
    return high, low


def dot(left, right):
    return lax.dot_general(left, right, (((1,), (0,)), ((), ())), preferred_element_type=F32)


def dot_t(left, right):
    return lax.dot_general(left, right, (((1,), (1,)), ((), ())), preferred_element_type=F32)


def t_dot(left, right):
    return lax.dot_general(left, right, (((0,), (0,)), ((), ())), preferred_element_type=F32)


def both(value):
    return value[:, :128] + value[:, 128:]


def iota(shape, dim):
    return lax.broadcasted_iota(jnp.int32, shape, dim)


def flag(condition):
    return jnp.where(condition, 1.0, 0.0).astype(F32)


def kernel(
    low_ref, mid_ref, high_ref, in_ref, env_ref, up_ref, out_ref,
    energy_ref, force_ref,
    grid_s, rows_s, geo_s, w_first, w_cast, w_env, w_env_t, w_up, w_down, w_rad, w_out,
    lat_s, slope_s, harm_s, msg_s, feat_s, dfeat_s, dlat_s, hout_s, back_s, vec_s,
    dfi_s, dfj_s, hot_c_s, hot_a_s, hot_at_s,
):
    col0 = lax.axis_index("xy") * 2
    first_row = (lax.axis_index("gz") % 2) * 2 + 1

    lane = iota((128, 128), 1)
    sub = iota((128, 128), 0)
    w_in = in_ref[...]
    wr_hi, wr_lo = halves(w_in[0:8])
    wi_hi, wi_lo = halves(w_in[8:16])
    wj_hi, wj_lo = halves(w_in[16:24])
    lane8 = iota((8, 128), 1)
    sub8 = iota((8, 128), 0)
    spread = flag((lane8 // CH) == (sub8 % 4))
    first = jnp.concatenate(
        [x.astype(F32) for x in (wr_hi, wr_hi, wr_lo, wi_hi, wi_lo, wj_hi, wj_lo)], axis=0
    )
    w_first[0:56, 0:128] = first.astype(BF16)
    w_first[0:64, 128:256] = jnp.concatenate([jnp.zeros((56, 128), F32), spread], axis=0).astype(BF16)
    w_first[48:64, 0:128] = jnp.concatenate([wj_lo.astype(F32), jnp.zeros((8, 128), F32)], axis=0).astype(BF16)
    zero8 = jnp.zeros((8, 128), F32)
    for block, table in enumerate(
        (
            flag(sub8 == 2),
            flag(sub8 == 3),
            flag(sub8 == 4),
            flag((sub8 == 5) | (sub8 == 6)),
        )
    ):
        w_cast[:, 128 * block : 128 * block + 128] = jnp.concatenate([zero8, table], axis=0).astype(BF16)
    env = env_ref[...]
    env_hi, env_lo = halves(env)
    tile = flag((iota((CH, 128), 1) % CH) == iota((CH, 128), 0)).astype(BF16)
    env4_hi = dot(env_hi, tile)
    env4_lo = dot(env_lo, tile)
    zero = jnp.zeros((128, 128), BF16)
    w_env[0:128, 0:128] = env4_hi.astype(BF16)
    w_env[0:128, 128:256] = env4_lo.astype(BF16)
    w_env[128:256, 0:128] = env4_hi.astype(BF16)
    w_env[128:256, 128:256] = zero
    env4_hi_t = jnp.transpose(env4_hi).astype(BF16)
    env4_lo_t = jnp.transpose(env4_lo).astype(BF16)
    w_env_t[0:128, 0:128] = env4_hi_t
    w_env_t[0:128, 128:256] = env4_lo_t
    w_env_t[128:256, 0:128] = env4_hi_t
    w_env_t[128:256, 128:256] = zero
    up = up_ref[...]
    up_l = up[0:128]
    up_p = jnp.concatenate([up[128:160]] * 4, axis=0)
    for base, block in ((0, up_l), (256, up_p)):
        hi, lo = halves(block)
        w_up[base : base + 128, 0:128] = hi
        w_up[base : base + 128, 128:256] = lo
        w_up[base + 128 : base + 256, 0:128] = hi
        w_up[base + 128 : base + 256, 128:256] = zero
        hi, lo = halves(jnp.transpose(block))
        w_down[0:128, base : base + 128] = hi
        w_down[128:256, base : base + 128] = hi
        w_down[0:128, base + 128 : base + 256] = lo
        w_down[128:256, base + 128 : base + 256] = zero
    z8 = jnp.zeros((8, 128), F32)
    wr_hi32 = wr_hi.astype(F32)
    wr_lo32 = wr_lo.astype(F32)
    ones4 = flag((lane8 // CH) == sub8)
    for block, parts in enumerate(
        ((wr_hi32, wr_lo32, z8, z8), (wr_hi32, z8, z8, z8), (z8, z8, ones4, z8), (z8, z8, ones4, z8))
    ):
        w_rad[:, 128 * block : 128 * block + 128] = jnp.concatenate(parts, axis=0).astype(BF16)
    out_row = out_ref[...]
    out_hi, out_lo = halves(out_row)
    out_hi32 = out_hi.astype(F32)
    out_lo32 = out_lo.astype(F32)
    z1 = jnp.zeros((1, 128), F32)
    pad14 = jnp.zeros((14, 128), F32)
    w_out[:, 0:128] = jnp.concatenate([out_hi32, out_lo32, pad14], axis=0).astype(BF16)
    w_out[:, 128:256] = jnp.concatenate([out_hi32, z1, pad14], axis=0).astype(BF16)

    for source, start in ((low_ref, 0), (mid_ref, 4), (high_ref, 8)):
        for peer in range(8):
            for row in range(2):
                for col in range(2):
                    place = ((start + peer // 4 * 2 + row) * COLS + peer % 4 * 2 + col) * 8
                    grid_s[place : place + 8, :] = source[peer, row, col]

    def quantity(row, which):
        return grid_s[pl.ds((first_row + row) * 64 + which, 8, stride=8), :]

    tables = [[quantity(row, which) for which in range(4)] for row in range(8)]
    for f in range(6):
        center = quantity(f + 1, 4)
        other = quantity(f + 1, 5)
        count = quantity(f + 1, 6)
        center_i = center.astype(jnp.int32)
        other_i = other.astype(jnp.int32)
        place = other_i // 128
        atom = other_i % 128
        at_i = [jnp.take_along_axis(tables[f + 1][which], center_i, axis=1) for which in range(4)]
        at_j = [jnp.zeros((8, 128), F32) for _ in range(4)]
        for offset in range(9):
            dr, dc = offset // 3 - 1, offset % 3 - 1
            here = place == offset
            for which in range(4):
                table = tables[f + 1 + dr][which]
                if dc:
                    table = pltpu.roll(table, (-dc) % 8, 0)
                value = jnp.take_along_axis(table, atom, axis=1)
                if which == 0:
                    value = value + float(dr)
                if which == 1:
                    value = value + float(dc)
                at_j[which] = jnp.where(here, value, at_j[which])
        dz, dx, dy = (at_j[which] - at_i[which] for which in range(3))
        distance = jnp.sqrt(dz * dz + dx * dx + dy * dy + SOFTEN)
        inverse = 1.0 / distance
        scaled = distance * (1.0 / CUTOFF)
        inner = 1.0 - scaled * scaled
        envelope = inner * inner
        slope = (-4.0 / CUTOFF) * inner * scaled
        live = flag(iota((8, 128), 1).astype(F32) < count)
        angle = PI * scaled
        sine, cosine = jnp.sin(angle), jnp.cos(angle)
        base = f * COLS * 32

        def put(which, value):
            rows_s[pl.ds(base + which, 8, stride=32), :] = value

        def split_put(which, gap, value):
            high = value.astype(BF16).astype(F32)
            put(which, high)
            put(which + gap, value - high)

        s_old, s_now = jnp.zeros_like(sine), sine
        c_old, c_now = jnp.ones_like(sine), cosine
        scale = inverse * envelope
        slope_scale = inverse * slope - inverse * scale
        for k in range(1, NB + 1):
            split_put(k - 1, 8, s_now * scale)
            geo_s[f, k - 1] = (k * PI / CUTOFF) * c_now * scale + s_now * slope_scale
            s_old, s_now = s_now, 2.0 * cosine * s_now - s_old
            c_old, c_now = c_now, 2.0 * cosine * c_now - c_old
        for m, value in enumerate((live, live * dz * inverse, live * dx * inverse, live * dy * inverse)):
            split_put(16 + m, 4, value)
        put(24, at_i[3])
        put(25, at_j[3])
        put(26, center)
        put(27, atom.astype(F32))
        put(28, place.astype(F32))
        split_put(29, 1, envelope * live)
        put(31, live)
        for which, value in enumerate((dz, dx, dy, inverse, live, slope, envelope)):
            geo_s[f, 8 + which] = value

    def slot(f, i):
        return f * COLS + ((col0 + (i + COLS - 2)) & (COLS - 1))

    def bin_rows(f, i, first, size):
        return rows_s[pl.ds(slot(f, i) * 32 + first, size), :]

    lanes = iota((128, 128), 1).astype(F32).astype(BF16)
    subs = iota((128, 128), 0).astype(F32).astype(BF16)
    one = jnp.ones((128, 128), BF16)

    def hot_rows(row):
        wide = jnp.broadcast_to(row, (128, 128)).astype(BF16)
        return jnp.where(wide == subs, one, zero)

    def feature_group(f, cols):
        inputs = []
        for i in cols:
            rows = bin_rows(f, i, 0, 32)
            spec_i = flag(rows[24:25] == iota((8, 128), 0).astype(F32))
            spec_j = flag(rows[25:26] == iota((8, 128), 0).astype(F32))
            inputs.append(jnp.concatenate(
                [rows[0:16], rows[0:8], spec_i, spec_i, spec_j, spec_j, rows[16:24]], axis=0
            ).astype(BF16))
        mixed = t_dot(jnp.concatenate(inputs, axis=1), w_first[...])
        pre, harm = mixed[:, :128], mixed[:, 128:]
        gate = 0.5 + 0.5 * jnp.tanh(0.5 * pre)
        latent = pre * gate
        lat = jnp.concatenate(halves(latent), axis=1)
        weights = both(dot(lat, w_env[...]))
        slope = gate + latent * (1.0 - gate)
        high, low = halves(weights * harm)
        for n, i in enumerate(cols):
            part = slice(128 * n, 128 * n + 128)
            message = jnp.concatenate([high[part], low[part]], axis=0)
            hot = hot_rows(bin_rows(f, i, 26, 1))
            feat = dot(jnp.concatenate([hot, hot], axis=1), message)
            lat_s[f, i] = lat[part]
            feat_s[f, i] = feat.astype(BF16)
            if 1 <= i <= 4:
                slope_s[f, i - 1] = slope[part]
                harm_s[f, i - 1] = harm[part]
                msg_s[f, i - 1] = weights[part]

    def feature_step(f, carry):
        for group in FEATURE_GROUPS:
            feature_group(f, group)
        return carry

    lax.fori_loop(0, 6, feature_step, 0)

    def cast(f, i):
        return t_dot(bin_rows(f, i, 16, 16).astype(BF16), w_cast[...])

    def energy_group(f, cols, reach, inside_row):
        feat_i, feat_j, weight, hots = [], [], [], []
        for i in cols:
            inside = inside_row and 1 <= i <= 4
            wide = cast(f, i)
            narrow = wide[:, :384].astype(BF16)
            center, atom, place = narrow[:, :128], narrow[:, 128:256], narrow[:, 256:]
            weight.append(wide[:, 384:])
            hot_c = jnp.where(center == lanes, one, zero)
            hot_a = jnp.where(atom == lanes, one, zero)
            feat_i.append(dot(hot_c, feat_s[f, i]))
            columns, tables_j = [], []
            for target, code in reach:
                for dc in (-1, 0, 1):
                    if inside or 1 <= i + dc <= 4:
                        columns.append(jnp.where(place == jnp.asarray(code + (dc + 1), F32).astype(BF16), hot_a, zero))
                        tables_j.append(feat_s[target, i + dc])
            feat_j.append(dot(jnp.concatenate(columns, axis=1), jnp.concatenate(tables_j, axis=0)))
            hots.append(hot_c)
            if inside:
                hot_c_s[f, i - 1] = hot_c
                hot_a_s[f, i - 1] = hot_a
            hot_at_s[f, i] = hot_rows(bin_rows(f, i, 27, 1))
        feat_i = jnp.concatenate(feat_i, axis=0)
        feat_j = jnp.concatenate(feat_j, axis=0)
        weight = jnp.concatenate(weight, axis=0)
        lat = jnp.concatenate([lat_s[f, i] for i in cols], axis=0)
        prod = jnp.concatenate(halves(feat_i * feat_j), axis=1)
        pre = both(dot(jnp.concatenate([lat, prod], axis=1), w_up[...]))
        gate = 0.5 + 0.5 * jnp.tanh(0.5 * pre)
        hidden = pre * gate
        d_pre = out_ref[...] * (gate + hidden * (1.0 - gate)) * weight
        d_pre = jnp.concatenate(halves(d_pre), axis=1)
        within = inside_row and 1 <= cols[0] <= 4
        if within:
            down = dot(d_pre, w_down[...])
            d_lat = both(down[:, :256])
            d_prod = both(down[:, 256:])
            hid = jnp.concatenate(halves(hidden), axis=1)
            readout = dot_t(w_out[...], hid)
            d_i = (d_prod * feat_j).astype(BF16)
        else:
            d_prod = both(dot(d_pre, w_down[:, 256:]))
        d_j = (d_prod * feat_i).astype(BF16)
        for n, i in enumerate(cols):
            part = slice(128 * n, 128 * n + 128)
            dfj_s[f, i] = d_j[part]
            if within:
                dfi_s[f, i - 1] = d_i[part]
                dlat_s[f, i - 1] = d_lat[part]
                value = readout[0:1, part] + readout[1:2, part]
                hout_s[pl.ds((f * 4 + (i - 1)) * 8, 8), :] = jnp.broadcast_to(value, (8, 128))
                if i in (2, 3):
                    rows = bin_rows(f, i, 24, 8)
                    edge = value * (rows[5:6] + rows[6:7])
                    high = edge.astype(BF16).astype(F32)
                    parts = jnp.concatenate([high, edge - high, jnp.zeros((14, 128), F32)], axis=0)
                    summed = dot(parts.astype(BF16), hots[n])
                    energy_ref[jnp.clip(f - 2, 0, 1), pl.ds(i - 2, 1), :] = jnp.where(
                        (f == 2) | (f == 3), summed[0:1] + summed[1:2],
                        energy_ref[jnp.clip(f - 2, 0, 1), pl.ds(i - 2, 1), :])

    def energy_step(f, carry):
        reach = [(f + dr, 3.0 * (dr + 1)) for dr in (-1, 0, 1)]
        for group in ENERGY_GROUPS:
            energy_group(f, group, reach, True)
        return carry

    def rim_step(t, carry):
        for group in RIM_GROUPS:
            energy_group(5 * t, group, [(1 + 3 * t, 6.0 - 6.0 * t.astype(F32))], False)
        return carry

    energy_ref[...] = jnp.zeros_like(energy_ref)
    lax.fori_loop(1, 5, energy_step, 0)
    lax.fori_loop(0, 2, rim_step, 0)

    def backward_group(f, cols):
        d_msg = []
        for i in cols:
            columns, terms = [hot_rows(bin_rows(f, i, 26, 1))], [dfi_s[f, i - 1]]
            for dr in (-1, 0, 1):
                for dc in (-1, 0, 1):
                    code = float(3 * (1 - dr) + (1 - dc))
                    mask = flag(bin_rows(f + dr, i + dc, 28, 1) == code)
                    mask = jnp.broadcast_to(mask, (128, 128)).astype(BF16)
                    columns.append(hot_at_s[f + dr, i + dc] * mask)
                    terms.append(dfj_s[f + dr, i + dc])
            d_feat = dot(jnp.concatenate(columns, axis=1), jnp.concatenate(terms, axis=0))
            hot = hot_c_s[f, i - 1]
            d_msg.append(dot(jnp.concatenate([hot, hot], axis=1), jnp.concatenate(halves(d_feat), axis=0)))
        d_msg = jnp.concatenate(d_msg, axis=0)
        gather = lambda ref: jnp.concatenate([ref[f, i - 1] for i in cols], axis=0)
        d_weight = jnp.concatenate(halves(d_msg * gather(harm_s)), axis=1)
        d_lat = both(dot(d_weight, w_env_t[...])) + gather(dlat_s)
        d_pre = jnp.concatenate(
            halves(d_lat * gather(slope_s)) + halves(d_msg * gather(msg_s)), axis=1
        )
        rows = dot_t(w_rad[...], d_pre)
        result = jnp.concatenate([rows[0:8] + rows[8:16], rows[16:24]], axis=0)
        for n, i in enumerate(cols):
            back_s[pl.ds(slot(f, i) * 16, 16), :] = result[:, 128 * n : 128 * n + 128]

    def backward_step(f, carry):
        for group in BACK_GROUPS:
            backward_group(f, group)
        return carry

    back_s[...] = jnp.zeros_like(back_s)
    lax.fori_loop(1, 5, backward_step, 0)

    for f in range(1, 5):
        def got(which):
            return back_s[pl.ds(f * COLS * 16 + which, 8, stride=16), :]

        dz, dx, dy, inverse, live, slope = (geo_s[f, 8 + which] for which in range(6))
        d_dist = jnp.zeros((8, 128), F32)
        for k in range(NB):
            d_dist = d_dist + got(k) * geo_s[f, k]
        readout = jnp.zeros((8, 128), F32)
        col = iota((8, 128), 0)
        for i in range(1, 5):
            value = hout_s[(f * 4 + i - 1) * 8 : (f * 4 + i - 1) * 8 + 8, :]
            readout = jnp.where(col == ((col0 + (i + COLS - 2)) & (COLS - 1)), value, readout)
        d_dist = d_dist + readout * live * slope
        hz, hx, hy = (got(8 + m) * live for m in (1, 2, 3))
        d_dist = d_dist - (hz * dz + hx * dx + hy * dy) * inverse * inverse
        along = d_dist * inverse
        for axis, (delta, own) in enumerate(((dz, hz), (dx, hx), (dy, hy))):
            value = along * delta + own * inverse
            high = value.astype(BF16).astype(F32)
            vec_s[pl.ds(f * COLS * 8 + 2 * axis, 8, stride=8), :] = high
            vec_s[pl.ds(f * COLS * 8 + 2 * axis + 1, 8, stride=8), :] = value - high
        for spare in (6, 7):
            vec_s[pl.ds(f * COLS * 8 + spare, 8, stride=8), :] = jnp.zeros((8, 128), F32)

    total = [[jnp.zeros((8, 128), F32) for _ in range(2)] for _ in range(2)]
    for f in range(1, 5):
        for i in range(1, 5):
            vec = vec_s[pl.ds(slot(f, i) * 8, 8), :]
            place = bin_rows(f, i, 28, 1)
            targets = [(dr, dc) for dr in (-1, 0, 1) for dc in (-1, 0, 1) if 2 <= i + dc <= 3 and 2 <= f + dr <= 3]
            parts = [vec * flag(place == float((dr + 1) * 3 + dc + 1)) for dr, dc in targets]
            if len(parts) % 2:
                parts.append(jnp.zeros((8, 128), F32))
            moved = dot(jnp.concatenate(parts, axis=0).astype(BF16), hot_a_s[f, i - 1])
            for index, (dr, dc) in enumerate(targets):
                total[f + dr - 2][i + dc - 2] -= moved[8 * index : 8 * index + 8]
            if i in (2, 3) and f in (2, 3):
                centered = jnp.concatenate([vec, jnp.zeros((8, 128), F32)], axis=0).astype(BF16)
                total[f - 2][i - 2] += dot(centered, hot_c_s[f, i - 1])[0:8]
    for row in range(2):
        for col in range(2):
            value = total[row][col]
            for axis in range(3):
                force_ref[axis, row, pl.ds(col, 1), :] = (
                    value[2 * axis : 2 * axis + 1] + value[2 * axis + 1 : 2 * axis + 2]
                )


FEATURE_GROUPS = ((0, 1, 2, 3, 4, 5),)
ENERGY_GROUPS = ((1, 2, 3, 4), (0, 5))
RIM_GROUPS = ((0, 1, 2, 3, 4, 5),)
BACK_GROUPS = ((1, 2, 3, 4),)


def compute(low, mid, high, in_weight, env_weight, up_weight, out_weight):
    return pl.pallas_call(
        kernel,
        out_shape=(
            jax.ShapeDtypeStruct((2, 2, 128), F32),
            jax.ShapeDtypeStruct((3, 2, 2, 128), F32),
        ),
        in_specs=[pl.BlockSpec(memory_space=pltpu.VMEM)] * 7,
        out_specs=[pl.BlockSpec(memory_space=pltpu.VMEM)] * 2,
        scratch_shapes=[
            pltpu.VMEM((12 * COLS * 8, 128), F32),
            pltpu.VMEM((6 * COLS * 32, 128), F32),
            pltpu.VMEM((6, 16, COLS, 128), F32),
            pltpu.VMEM((64, 256), BF16),
            pltpu.VMEM((16, 512), BF16),
            pltpu.VMEM((256, 256), BF16),
            pltpu.VMEM((256, 256), BF16),
            pltpu.VMEM((512, 256), BF16),
            pltpu.VMEM((256, 512), BF16),
            pltpu.VMEM((32, 512), BF16),
            pltpu.VMEM((16, 256), BF16),
            pltpu.VMEM((6, 6, 128, 256), BF16),
            pltpu.VMEM((6, 4, 128, 128), F32),
            pltpu.VMEM((6, 4, 128, 128), F32),
            pltpu.VMEM((6, 4, 128, 128), F32),
            pltpu.VMEM((6, 6, 128, 128), BF16),
            pltpu.VMEM((8, 128), F32),
            pltpu.VMEM((6, 4, 128, 128), F32),
            pltpu.VMEM((6 * 4 * 8, 128), F32),
            pltpu.VMEM((6 * COLS * 16, 128), F32),
            pltpu.VMEM((6 * COLS * 8, 128), F32),
            pltpu.VMEM((6, 4, 128, 128), BF16),
            pltpu.VMEM((6, 6, 128, 128), BF16),
            pltpu.VMEM((6, 4, 128, 128), BF16),
            pltpu.VMEM((6, 4, 128, 128), BF16),
            pltpu.VMEM((6, 6, 128, 128), BF16),
        ],
        compiler_params=pltpu.CompilerParams(vmem_limit_bytes=40 * 1024 * 1024),
        name="potential",
    )(low, mid, high, in_weight, env_weight, up_weight, out_weight)


def pack_kernel(coords_ref, species_ref, centers_ref, others_ref, live_ref, packed_ref):
    for row in range(2):
        for col in range(2):
            at = pl.ds(col, 1)
            tile = jnp.concatenate(
                [coords_ref[axis, row, at, :] for axis in range(3)]
                + [ref[row, at, :].astype(F32) for ref in (species_ref, centers_ref, others_ref)]
                + [jnp.full((1, 128), live_ref[row, col], jnp.int32).astype(F32), jnp.zeros((1, 128), F32)],
                axis=0,
            )
            for peer in range(8):
                packed_ref[peer, row, col] = tile


def pack(coords, species, centers, others, live_count):
    return pl.pallas_call(
        pack_kernel,
        out_shape=jax.ShapeDtypeStruct((8, 2, 2, 8, 128), F32),
        in_specs=[pl.BlockSpec(memory_space=pltpu.VMEM)] * 4 + [pl.BlockSpec(memory_space=pltpu.SMEM)],
        out_specs=pl.BlockSpec(memory_space=pltpu.VMEM),
        name="pack",
    )(coords, species, centers, others, live_count)


def shift(value, axis, step):
    count = lax.axis_size(axis)
    return lax.ppermute(value, axis, [(i, (i + step) % count) for i in range(count)])


def body(
    coords, species, centers, others, live_count, in_weight, env_weight, up_weight, out_weight
):
    packed = pack(coords, species, centers, others, live_count)
    depth, width = lax.axis_size("gz"), lax.axis_size("xy")
    chips = [
        [(2 * chip + core) * width + place for core in range(2) for place in range(width)]
        for chip in range(depth // 2)
    ]
    mid = lax.all_to_all(packed, ("gz", "xy"), 0, 0, tiled=True, axis_index_groups=chips)
    low = shift(mid, "gz", 2)
    high = shift(mid, "gz", -2)
    return compute(low, mid, high, in_weight, env_weight, up_weight, out_weight.reshape(1, -1))


def solution(mesh):
    in_specs = (
        P(None, "gz", "xy", None),
        P("gz", "xy", None),
        P("gz", "xy", None),
        P("gz", "xy", None),
        P("gz", "xy"),
        P(),
        P(),
        P(),
        P(),
    )
    out_specs = (P("gz", "xy", None), P(None, "gz", "xy", None))
    return jax.shard_map(body, mesh=mesh, in_specs=in_specs, out_specs=out_specs, check_vma=False)
```

time: 136 us -> 74.9 us (0.55)
  the two profiles are of different devices: /device:TPU:24 before, /device:TPU:1 now
where the time goes in v1:
time: 74.9 us; the launch traced here: 74.5 us
  Pallas kernels  25.6 us (34%)
  blocking collectives  20.5 us (27%)
  starting transfers between devices  14.8 us (20%)
  waiting for transfers between devices  12.8 us (17%)
    pallas_call x1, Pallas kernels, compute(): pl.pallas_call(kernel, out_shape=(jax.ShapeDtypeStruct((2, 2, 128), F32),...  24.2 us
    all_to_all x1, blocking collectives, body(): lax.all_to_all(packed, ('gz', 'xy'), 0, 0, tiled=True, axis_index_groups=...  20.5 us
    ppermute x2, starting transfers between devices, shift(): lax.ppermute(value, axis, [(i, (i + step) % count) for i in range(count)])  14.8 us
    ppermute x2, waiting for transfers between devices, shift(): lax.ppermute(value, axis, [(i, (i + step) % count) for i in range(count)])  12.8 us
  transfers between devices with their start and end apart: 2, of which 2 were waited for; matrix products, arithmetic and copies ran while one was open for 0% of the time, Pallas kernels for 0%

profile of v1, /device:TPU:1, one launch (start us, length us, event | category | flops | bytes accessed | tf_op | source)
XLA Modules:
  0.0 74.5 jit_solution(1359733169968465939)
XLA Ops:
  0.6 1.5 %pack.1 = f32[8,2,2,8,128]{4,3,2,1,0:T(8,128)} custom-call(f32[3,2,2,128]{3,2,1,0:T(2,128)} %coords_ref.1, s32[2,2,128]{2,1,0:T(2,128)} %species_ref.1, s32[2,2,128]{2,1,0:T(2,128)} %centers_ref.1, s32[2,2,128]{2,1,0:T(2,128)} %others_ref.1, s32[2,2]{1,0:T(2,128)} %live_ref.1), custom_call_target="tpu_custom_call" | custom-call | tf_op jit(solution)/shard_map/pack/pallas_call | solution.py:483
  2.1 0.0 copy-start.3
  2.1 0.0 copy-start.1
  2.1 20.5 %all_to_all.5.mid_ref = f32[8,2,2,8,128]{4,3,2,1,0:T(8,128)S(1)} all-to-all(f32[8,2,2,8,128]{4,3,2,1,0:T(8,128)} %pack.1), channel_id=1, replica_groups={{0,1,2,3,4,5,6,7},{8,9,10,11,12,13,14,15},{16,17,18,19,20,21,22,23},{24..., dimensions={0} | all-to-all | bytes 262144 | tf_op jit(solution)/shard_map/all_to_all | solution.py:506
  22.6 0.0 copy-start
  22.6 12.9 %collective-permute-start.1 = (f32[8,2,2,8,128]{4,3,2,1,0:T(8,128)S(1)}, f32[8,2,2,8,128]{4,3,2,1,0:T(8,128)S(1)}, u32[]{:S(2)}, u32[]{:S(2)}) collective-permute-start(f32[8,2,2,8,128]{4,3,2,1,0:T(8,128)S(1)} %all_to_all.5.mid_ref), channel_id=1, source_target_pairs={{0,760},{4,764},{8,0},{12,4},{16,8},{20,12},{24,16},{28,20},{32,24... | collective-permute-start | bytes 393224 | tf_op jit(solution)/shard_map/ppermute | solution.py:494
  35.5 1.9 %collective-permute-start = (f32[8,2,2,8,128]{4,3,2,1,0:T(8,128)S(1)}, f32[8,2,2,8,128]{4,3,2,1,0:T(8,128)S(1)}, u32[]{:S(2)}, u32[]{:S(2)}) collective-permute-start(f32[8,2,2,8,128]{4,3,2,1,0:T(8,128)S(1)} %all_to_all.5.mid_ref), channel_id=1, source_target_pairs={{0,8},{4,12},{8,16},{12,20},{16,24},{20,28},{24,32},{28,36},{32,40... | collective-permute-start | bytes 393224 | tf_op jit(solution)/shard_map/ppermute | solution.py:494
  37.4 0.0 copy-done.3
  37.4 0.1 copy.11.env_ref
  37.5 0.0 copy-start.2
  37.5 0.4 collective-permute-done.1.high_ref
  37.9 12.4 %collective-permute-done.low_ref = f32[8,2,2,8,128]{4,3,2,1,0:T(8,128)S(1)} collective-permute-done((f32[8,2,2,8,128]{4,3,2,1,0:T(8,128)S(1)}, f32[8,2,2,8,128]{4,3,2,1,0:T(8,128)S(1)}, u32[]{:S(2)}, u32[]{:S(2)}) %collective-permute-start) | collective-permute-done | bytes 131104 | tf_op jit(solution)/shard_map/ppermute | solution.py:494
  50.3 0.0 copy-done.1
  50.3 0.0 copy-done
  50.3 0.0 copy-done.2
  50.3 24.2 %potential.1 = (f32[2,2,128]{2,1,0:T(2,128)}, f32[3,2,2,128]{3,2,1,0:T(2,128)}) custom-call(f32[8,2,2,8,128]{4,3,2,1,0:T(8,128)S(1)} %collective-permute-done.low_ref, f32[8,2,2,8,128]{4,3,2,1,0:T(8,128)S(1)} %all_to_all.5.mid_ref, f32[8,2,2,8,128]{4,3,2,1,0:T(8,128)S(1)} %collective-permute-done.1.high_ref, f32[24,128]{1,0:T(8,128)S(1)} %copy-done.1, ...), custom_call_target="tpu_custom_call" | custom-call | tf_op jit(solution)/shard_map/potential/pallas_call | solution.py:427
Async XLA Ops:
  2.1 35.3 %copy-start.3 = (f32[128,32]{0,1:T(8,128)S(1)}, f32[128,32]{0,1:T(8,128)}, u32[]{:S(2)}) copy-start(f32[128,32]{0,1:T(8,128)} %param.15) | copy-start | bytes 49156
  2.1 48.2 %copy-start.1 = (f32[24,128]{1,0:T(8,128)S(1)}, f32[24,128]{1,0:T(8,128)}, u32[]{:S(2)}) copy-start(f32[24,128]{1,0:T(8,128)} %in_ref.1) | copy-start | bytes 36868
  22.6 27.7 %copy-start = (f32[160,128]{1,0:T(8,128)S(1)}, f32[160,128]{1,0:T(8,128)}, u32[]{:S(2)}) copy-start(f32[160,128]{1,0:T(8,128)} %up_ref.1) | copy-start | bytes 245764
  22.6 15.3 %collective-permute-start.1 = (f32[8,2,2,8,128]{4,3,2,1,0:T(8,128)S(1)}, f32[8,2,2,8,128]{4,3,2,1,0:T(8,128)S(1)}, u32[]{:S(2)}, u32[]{:S(2)}) collective-permute-start(f32[8,2,2,8,128]{4,3,2,1,0:T(8,128)S(1)} %all_to_all.5.mid_ref), channel_id=1, source_target_pairs={{0,760},{4,764},{8,0},{12,4},{16,8},{20,12},{24,16},{28,20},{32,24... | collective-permute-start | bytes 393224 | tf_op jit(solution)/shard_map/ppermute | solution.py:494
  35.5 14.8 %collective-permute-start = (f32[8,2,2,8,128]{4,3,2,1,0:T(8,128)S(1)}, f32[8,2,2,8,128]{4,3,2,1,0:T(8,128)S(1)}, u32[]{:S(2)}, u32[]{:S(2)}) collective-permute-start(f32[8,2,2,8,128]{4,3,2,1,0:T(8,128)S(1)} %all_to_all.5.mid_ref), channel_id=1, source_target_pairs={{0,8},{4,12},{8,16},{12,20},{16,24},{20,28},{24,32},{28,36},{32,40... | collective-permute-start | bytes 393224 | tf_op jit(solution)/shard_map/ppermute | solution.py:494
  37.5 12.8 %copy-start.2 = (f32[128]{0:T(128)S(1)}, f32[128]{0:T(128)}, u32[]{:S(2)}) copy-start(f32[128]{0:T(128)} %param.17) | copy-start | bytes 1540

commit v2 on v1

--- a/solution.py
+++ b/solution.py
@@ -50,9 +50,9 @@
 def kernel(
     low_ref, mid_ref, high_ref, in_ref, env_ref, up_ref, out_ref,
     energy_ref, force_ref,
-    grid_s, rows_s, geo_s, w_first, w_cast, w_env, w_env_t, w_up, w_down, w_rad, w_out,
+    grid_s, rows_s, geo_s, w_first, w_env, w_env_t, w_up, w_down, w_rad, w_out,
     lat_s, slope_s, harm_s, msg_s, feat_s, dfeat_s, dlat_s, hout_s, back_s, vec_s,
-    dfi_s, dfj_s, hot_c_s, hot_a_s, hot_at_s,
+    dfi_s, dfj_s, hot_c_s, hot_a_s, hot_at_s, index_s, weight_s,
 ):
     col0 = lax.axis_index("xy") * 2
     first_row = (lax.axis_index("gz") % 2) * 2 + 1
@@ -69,10 +69,10 @@
     first = jnp.concatenate(
         [x.astype(F32) for x in (wr_hi, wr_hi, wr_lo, wi_hi, wi_lo, wj_hi, wj_lo)], axis=0
     )
-    w_first[0:56, 0:128] = first.astype(BF16)
-    w_first[0:64, 128:256] = jnp.concatenate([jnp.zeros((56, 128), F32), spread], axis=0).astype(BF16)
-    w_first[48:64, 0:128] = jnp.concatenate([wj_lo.astype(F32), jnp.zeros((8, 128), F32)], axis=0).astype(BF16)
-    zero8 = jnp.zeros((8, 128), F32)
+    w_first[:, 0:128] = jnp.concatenate([first, jnp.zeros((24, 128), F32)], axis=0).astype(BF16)
+    w_first[:, 128:256] = jnp.concatenate(
+        [jnp.zeros((56, 128), F32), spread, jnp.zeros((16, 128), F32)], axis=0
+    ).astype(BF16)
     for block, table in enumerate(
         (
             flag(sub8 == 2),
@@ -81,7 +81,9 @@
             flag((sub8 == 5) | (sub8 == 6)),
         )
     ):
-        w_cast[:, 128 * block : 128 * block + 128] = jnp.concatenate([zero8, table], axis=0).astype(BF16)
+        w_first[:, 128 * block + 256 : 128 * block + 384] = jnp.concatenate(
+            [jnp.zeros((64, 128), F32), table, jnp.zeros((8, 128), F32)], axis=0
+        ).astype(BF16)
     env = env_ref[...]
     env_hi, env_lo = halves(env)
     tile = flag((iota((CH, 128), 1) % CH) == iota((CH, 128), 0)).astype(BF16)
@@ -134,7 +136,8 @@
             for row in range(2):
                 for col in range(2):
                     place = ((start + peer // 4 * 2 + row) * COLS + peer % 4 * 2 + col) * 8
-                    grid_s[place : place + 8, :] = source[peer, row, col]
+                    size = source.shape[3]
+                    grid_s[place : place + size, :] = source[peer, row, col]
 
     def quantity(row, which):
         return grid_s[pl.ds((first_row + row) * 64 + which, 8, stride=8), :]
@@ -225,10 +228,12 @@
             spec_i = flag(rows[24:25] == iota((8, 128), 0).astype(F32))
             spec_j = flag(rows[25:26] == iota((8, 128), 0).astype(F32))
             inputs.append(jnp.concatenate(
-                [rows[0:16], rows[0:8], spec_i, spec_i, spec_j, spec_j, rows[16:24]], axis=0
+                [rows[0:16], rows[0:8], spec_i, spec_i, spec_j, spec_j, rows[16:32], jnp.zeros((8, 128), F32)],
+                axis=0,
             ).astype(BF16))
         mixed = t_dot(jnp.concatenate(inputs, axis=1), w_first[...])
-        pre, harm = mixed[:, :128], mixed[:, 128:]
+        pre, harm = mixed[:, :128], mixed[:, 128:256]
+        narrow = mixed[:, 256:640].astype(BF16)
         gate = 0.5 + 0.5 * jnp.tanh(0.5 * pre)
         latent = pre * gate
         lat = jnp.concatenate(halves(latent), axis=1)
@@ -241,6 +246,8 @@
             hot = hot_rows(bin_rows(f, i, 26, 1))
             feat = dot(jnp.concatenate([hot, hot], axis=1), message)
             lat_s[f, i] = lat[part]
+            index_s[f, i] = narrow[part]
+            weight_s[f, i] = mixed[part, 640:]
             feat_s[f, i] = feat.astype(BF16)
             if 1 <= i <= 4:
                 slope_s[f, i - 1] = slope[part]
@@ -254,17 +261,13 @@
 
     lax.fori_loop(0, 6, feature_step, 0)
 
-    def cast(f, i):
-        return t_dot(bin_rows(f, i, 16, 16).astype(BF16), w_cast[...])
-
     def energy_group(f, cols, reach, inside_row):
         feat_i, feat_j, weight, hots = [], [], [], []
         for i in cols:
             inside = inside_row and 1 <= i <= 4
-            wide = cast(f, i)
-            narrow = wide[:, :384].astype(BF16)
+            narrow = index_s[f, i]
             center, atom, place = narrow[:, :128], narrow[:, 128:256], narrow[:, 256:]
-            weight.append(wide[:, 384:])
+            weight.append(weight_s[f, i])
             hot_c = jnp.where(center == lanes, one, zero)
             hot_a = jnp.where(atom == lanes, one, zero)
             feat_i.append(dot(hot_c, feat_s[f, i]))
@@ -297,10 +300,10 @@
             d_prod = both(down[:, 256:])
             hid = jnp.concatenate(halves(hidden), axis=1)
             readout = dot_t(w_out[...], hid)
-            d_i = (d_prod * feat_j).astype(BF16)
+            d_i = jnp.concatenate(halves(d_prod * feat_j), axis=1)
         else:
             d_prod = both(dot(d_pre, w_down[:, 256:]))
-        d_j = (d_prod * feat_i).astype(BF16)
+        d_j = jnp.concatenate(halves(d_prod * feat_i), axis=1)
         for n, i in enumerate(cols):
             part = slice(128 * n, 128 * n + 128)
             dfj_s[f, i] = d_j[part]
@@ -345,7 +348,7 @@
                     mask = jnp.broadcast_to(mask, (128, 128)).astype(BF16)
                     columns.append(hot_at_s[f + dr, i + dc] * mask)
                     terms.append(dfj_s[f + dr, i + dc])
-            d_feat = dot(jnp.concatenate(columns, axis=1), jnp.concatenate(terms, axis=0))
+            d_feat = both(dot(jnp.concatenate(columns, axis=1), jnp.concatenate(terms, axis=0)))
             hot = hot_c_s[f, i - 1]
             d_msg.append(dot(jnp.concatenate([hot, hot], axis=1), jnp.concatenate(halves(d_feat), axis=0)))
         d_msg = jnp.concatenate(d_msg, axis=0)
@@ -436,8 +439,7 @@
             pltpu.VMEM((12 * COLS * 8, 128), F32),
             pltpu.VMEM((6 * COLS * 32, 128), F32),
             pltpu.VMEM((6, 16, COLS, 128), F32),
-            pltpu.VMEM((64, 256), BF16),
-            pltpu.VMEM((16, 512), BF16),
+            pltpu.VMEM((80, 768), BF16),
             pltpu.VMEM((256, 256), BF16),
             pltpu.VMEM((256, 256), BF16),
             pltpu.VMEM((512, 256), BF16),
@@ -454,11 +456,13 @@
             pltpu.VMEM((6 * 4 * 8, 128), F32),
             pltpu.VMEM((6 * COLS * 16, 128), F32),
             pltpu.VMEM((6 * COLS * 8, 128), F32),
-            pltpu.VMEM((6, 4, 128, 128), BF16),
-            pltpu.VMEM((6, 6, 128, 128), BF16),
+            pltpu.VMEM((6, 4, 128, 256), BF16),
+            pltpu.VMEM((6, 6, 128, 256), BF16),
             pltpu.VMEM((6, 4, 128, 128), BF16),
             pltpu.VMEM((6, 4, 128, 128), BF16),
             pltpu.VMEM((6, 6, 128, 128), BF16),
+            pltpu.VMEM((6, 6, 128, 384), BF16),
+            pltpu.VMEM((6, 6, 128, 128), F32),
         ],
         compiler_params=pltpu.CompilerParams(vmem_limit_bytes=40 * 1024 * 1024),
         name="potential",
@@ -505,7 +509,7 @@
     ]
     mid = lax.all_to_all(packed, ("gz", "xy"), 0, 0, tiled=True, axis_index_groups=chips)
     low = shift(mid, "gz", 2)
-    high = shift(mid, "gz", -2)
+    high = shift(mid[..., :7, :], "gz", -2)
     return compute(low, mid, high, in_weight, env_weight, up_weight, out_weight.reshape(1, -1))
 
 

time: 74.9 us -> 61.7 us (0.82)
  waiting for transfers between devices: 12.8 us -> 3.07 us
  Pallas kernels: 25.6 us -> 22.2 us
    ppermute x2, waiting for transfers between devices: 12.8 us -> 3.07 us  [shift(): lax.ppermute(value, axis, [(i, (i + step) % count) for i in range(count)])]
    pallas_call x1, Pallas kernels: 24.2 us -> 20.7 us  [compute(): pl.pallas_call(kernel, out_shape=(jax.ShapeDtypeStruct((2, 2, 128), F32),...]
where the time goes in v2:
time: 61.7 us; the launch traced here: 61.3 us
  Pallas kernels  22.2 us (36%)
  blocking collectives  20.5 us (33%)
  starting transfers between devices  14.8 us (24%)
  waiting for transfers between devices  3.07 us (5%)
  between operations  0.67 us (1%)
    pallas_call x1, Pallas kernels, compute(): pl.pallas_call(kernel, out_shape=(jax.ShapeDtypeStruct((2, 2, 128), F32),...  20.7 us
    all_to_all x1, blocking collectives, body(): lax.all_to_all(packed, ('gz', 'xy'), 0, 0, tiled=True, axis_index_groups=...  20.5 us
    ppermute x2, starting transfers between devices, shift(): lax.ppermute(value, axis, [(i, (i + step) % count) for i in range(count)])  14.8 us
    ppermute x2, waiting for transfers between devices, shift(): lax.ppermute(value, axis, [(i, (i + step) % count) for i in range(count)])  3.07 us
    pallas_call x1, Pallas kernels, pack(): pl.pallas_call(pack_kernel, out_shape=jax.ShapeDtypeStruct((8, 2, 2, 8, 1...  1.49 us
  transfers between devices with their start and end apart: 2, of which 2 were waited for; matrix products, arithmetic and copies ran while one was open for 0% of the time, Pallas kernels for 0%

profile of v2, /device:TPU:1, one launch (start us, length us, event | category | flops | bytes accessed | tf_op | source)
XLA Modules:
  0.0 61.3 jit_solution(11290039623607584235)
XLA Ops:
  0.6 1.5 %pack.1 = f32[8,2,2,8,128]{4,3,2,1,0:T(8,128)} custom-call(f32[3,2,2,128]{3,2,1,0:T(2,128)} %coords_ref.1, s32[2,2,128]{2,1,0:T(2,128)} %species_ref.1, s32[2,2,128]{2,1,0:T(2,128)} %centers_ref.1, s32[2,2,128]{2,1,0:T(2,128)} %others_ref.1, s32[2,2]{1,0:T(2,128)} %live_ref.1), custom_call_target="tpu_custom_call" | custom-call | tf_op jit(solution)/shard_map/pack/pallas_call | solution.py:487
  2.1 0.0 copy-start.3
  2.1 0.0 copy-start.1
  2.1 20.5 %all_to_all.5.mid_ref = f32[8,2,2,8,128]{4,3,2,1,0:T(8,128)S(1)} all-to-all(f32[8,2,2,8,128]{4,3,2,1,0:T(8,128)} %pack.1), channel_id=1, replica_groups={{0,1,2,3,4,5,6,7},{8,9,10,11,12,13,14,15},{16,17,18,19,20,21,22,23},{24..., dimensions={0} | all-to-all | bytes 262144 | tf_op jit(solution)/shard_map/all_to_all | solution.py:510
  22.6 0.0 copy-start
  22.6 2.0 %collective-permute-start = (f32[8,2,2,8,128]{4,3,2,1,0:T(8,128)S(1)}, f32[8,2,2,8,128]{4,3,2,1,0:T(8,128)S(1)}, u32[]{:S(2)}, u32[]{:S(2)}) collective-permute-start(f32[8,2,2,8,128]{4,3,2,1,0:T(8,128)S(1)} %all_to_all.5.mid_ref), channel_id=1, source_target_pairs={{0,8},{4,12},{8,16},{12,20},{16,24},{20,28},{24,32},{28,36},{32,40... | collective-permute-start | bytes 393224 | tf_op jit(solution)/shard_map/ppermute | solution.py:498
  24.6 12.8 %collective-permute-start.1 = (f32[8,2,2,7,128]{4,3,2,1,0:T(8,128)S(1)}, f32[8,2,2,7,128]{4,3,2,1,0:T(8,128)S(1)}, u32[]{:S(2)}, u32[]{:S(2)}) collective-permute-start(f32[8,2,2,7,128]{4,3,2,1,0:T(8,128)S(1)} %bitcast.2), channel_id=1, source_target_pairs={{0,760},{4,764},{8,0},{12,4},{16,8},{20,12},{24,16},{28,20},{32,24... | collective-permute-start | bytes 344072 | tf_op jit(solution)/shard_map/ppermute | solution.py:498
  37.4 0.0 copy-done.3
  37.4 0.1 copy.11.env_ref
  37.5 0.0 copy-start.2
  37.5 2.3 %collective-permute-done.1.high_ref = f32[8,2,2,7,128]{4,3,2,1,0:T(8,128)S(1)} collective-permute-done((f32[8,2,2,7,128]{4,3,2,1,0:T(8,128)S(1)}, f32[8,2,2,7,128]{4,3,2,1,0:T(8,128)S(1)}, u32[]{:S(2)}, u32[]{:S(2)}) %collective-permute-start.1) | collective-permute-done | bytes 114720 | tf_op jit(solution)/shard_map/ppermute | solution.py:498
  39.9 0.7 %collective-permute-done.low_ref = f32[8,2,2,8,128]{4,3,2,1,0:T(8,128)S(1)} collective-permute-done((f32[8,2,2,8,128]{4,3,2,1,0:T(8,128)S(1)}, f32[8,2,2,8,128]{4,3,2,1,0:T(8,128)S(1)}, u32[]{:S(2)}, u32[]{:S(2)}) %collective-permute-start) | collective-permute-done | bytes 131104 | tf_op jit(solution)/shard_map/ppermute | solution.py:498
  40.6 0.0 copy-done.1
  40.6 0.0 copy-done
  40.6 0.0 copy-done.2
  40.6 20.7 %potential.1 = (f32[2,2,128]{2,1,0:T(2,128)}, f32[3,2,2,128]{3,2,1,0:T(2,128)}) custom-call(f32[8,2,2,8,128]{4,3,2,1,0:T(8,128)S(1)} %collective-permute-done.low_ref, f32[8,2,2,8,128]{4,3,2,1,0:T(8,128)S(1)} %all_to_all.5.mid_ref, f32[8,2,2,7,128]{4,3,2,1,0:T(8,128)S(1)} %collective-permute-done.1.high_ref, f32[24,128]{1,0:T(8,128)S(1)} %copy-done.1, ...), custom_call_target="tpu_custom_call" | custom-call | tf_op jit(solution)/shard_map/potential/pallas_call | solution.py:430
Async XLA Ops:
  2.1 35.3 %copy-start.3 = (f32[128,32]{0,1:T(8,128)S(1)}, f32[128,32]{0,1:T(8,128)}, u32[]{:S(2)}) copy-start(f32[128,32]{0,1:T(8,128)} %param.15) | copy-start | bytes 49156
  2.1 38.5 %copy-start.1 = (f32[24,128]{1,0:T(8,128)S(1)}, f32[24,128]{1,0:T(8,128)}, u32[]{:S(2)}) copy-start(f32[24,128]{1,0:T(8,128)} %in_ref.1) | copy-start | bytes 36868
  22.6 18.0 %copy-start = (f32[160,128]{1,0:T(8,128)S(1)}, f32[160,128]{1,0:T(8,128)}, u32[]{:S(2)}) copy-start(f32[160,128]{1,0:T(8,128)} %up_ref.1) | copy-start | bytes 245764
  22.6 18.0 %collective-permute-start = (f32[8,2,2,8,128]{4,3,2,1,0:T(8,128)S(1)}, f32[8,2,2,8,128]{4,3,2,1,0:T(8,128)S(1)}, u32[]{:S(2)}, u32[]{:S(2)}) collective-permute-start(f32[8,2,2,8,128]{4,3,2,1,0:T(8,128)S(1)} %all_to_all.5.mid_ref), channel_id=1, source_target_pairs={{0,8},{4,12},{8,16},{12,20},{16,24},{20,28},{24,32},{28,36},{32,40... | collective-permute-start | bytes 393224 | tf_op jit(solution)/shard_map/ppermute | solution.py:498
  24.6 15.2 %collective-permute-start.1 = (f32[8,2,2,7,128]{4,3,2,1,0:T(8,128)S(1)}, f32[8,2,2,7,128]{4,3,2,1,0:T(8,128)S(1)}, u32[]{:S(2)}, u32[]{:S(2)}) collective-permute-start(f32[8,2,2,7,128]{4,3,2,1,0:T(8,128)S(1)} %bitcast.2), channel_id=1, source_target_pairs={{0,760},{4,764},{8,0},{12,4},{16,8},{20,12},{24,16},{28,20},{32,24... | collective-permute-start | bytes 344072 | tf_op jit(solution)/shard_map/ppermute | solution.py:498
  37.5 3.1 %copy-start.2 = (f32[128]{0:T(128)S(1)}, f32[128]{0:T(128)}, u32[]{:S(2)}) copy-start(f32[128]{0:T(128)} %param.17) | copy-start | bytes 1540

commit v3 on v2

--- a/solution.py
+++ b/solution.py
@@ -48,7 +48,7 @@
 
 
 def kernel(
-    low_ref, mid_ref, high_ref, in_ref, env_ref, up_ref, out_ref,
+    far_ref, mid_ref, near_ref, in_ref, env_ref, up_ref, out_ref,
     energy_ref, force_ref,
     grid_s, rows_s, geo_s, w_first, w_env, w_env_t, w_up, w_down, w_rad, w_out,
     lat_s, slope_s, harm_s, msg_s, feat_s, dfeat_s, dlat_s, hout_s, back_s, vec_s,
@@ -131,13 +131,14 @@
     w_out[:, 0:128] = jnp.concatenate([out_hi32, out_lo32, pad14], axis=0).astype(BF16)
     w_out[:, 128:256] = jnp.concatenate([out_hi32, z1, pad14], axis=0).astype(BF16)
 
-    for source, start in ((low_ref, 0), (mid_ref, 4), (high_ref, 8)):
+    odd = (lax.axis_index("gz") // 2) % 2
+    for source, start in ((far_ref, 8 * odd), (mid_ref, 4), (near_ref, 8 - 8 * odd)):
         for peer in range(8):
             for row in range(2):
                 for col in range(2):
-                    place = ((start + peer // 4 * 2 + row) * COLS + peer % 4 * 2 + col) * 8
+                    place = start * (COLS * 8) + ((peer // 4 * 2 + row) * COLS + peer % 4 * 2 + col) * 8
                     size = source.shape[3]
-                    grid_s[place : place + size, :] = source[peer, row, col]
+                    grid_s[pl.ds(pl.multiple_of(place, 8), size), :] = source[peer, row, col]
 
     def quantity(row, which):
         return grid_s[pl.ds((first_row + row) * 64 + which, 8, stride=8), :]
@@ -259,7 +260,8 @@
             feature_group(f, group)
         return carry
 
-    lax.fori_loop(0, 6, feature_step, 0)
+    for f in range(6):
+        feature_step(f, 0)
 
     def energy_group(f, cols, reach, inside_row):
         feat_i, feat_j, weight, hots = [], [], [], []
@@ -334,7 +336,8 @@
         return carry
 
     energy_ref[...] = jnp.zeros_like(energy_ref)
-    lax.fori_loop(1, 5, energy_step, 0)
+    for f in range(1, 5):
+        energy_step(f, 0)
     lax.fori_loop(0, 2, rim_step, 0)
 
     def backward_group(f, cols):
@@ -369,7 +372,8 @@
         return carry
 
     back_s[...] = jnp.zeros_like(back_s)
-    lax.fori_loop(1, 5, backward_step, 0)
+    for f in range(1, 5):
+        backward_step(f, 0)
 
     for f in range(1, 5):
         def got(which):
@@ -421,12 +425,12 @@
 
 
 FEATURE_GROUPS = ((0, 1, 2, 3, 4, 5),)
-ENERGY_GROUPS = ((1, 2, 3, 4), (0, 5))
+ENERGY_GROUPS = ((0, 5), (1, 2, 3, 4))
 RIM_GROUPS = ((0, 1, 2, 3, 4, 5),)
 BACK_GROUPS = ((1, 2, 3, 4),)
 
 
-def compute(low, mid, high, in_weight, env_weight, up_weight, out_weight):
+def compute(far, mid, near, in_weight, env_weight, up_weight, out_weight):
     return pl.pallas_call(
         kernel,
         out_shape=(
@@ -466,7 +470,7 @@
         ],
         compiler_params=pltpu.CompilerParams(vmem_limit_bytes=40 * 1024 * 1024),
         name="potential",
-    )(low, mid, high, in_weight, env_weight, up_weight, out_weight)
+    )(far, mid, near, in_weight, env_weight, up_weight, out_weight)
 
 
 def pack_kernel(coords_ref, species_ref, centers_ref, others_ref, live_ref, packed_ref):
@@ -493,9 +497,8 @@
     )(coords, species, centers, others, live_count)
 
 
-def shift(value, axis, step):
-    count = lax.axis_size(axis)
-    return lax.ppermute(value, axis, [(i, (i + step) % count) for i in range(count)])
+def swap(value, count, first):
+    return lax.ppermute(value, "gz", [(i, (((i + first) ^ 2) - first) % count) for i in range(count)])
 
 
 def body(
@@ -508,9 +511,9 @@
         for chip in range(depth // 2)
     ]
     mid = lax.all_to_all(packed, ("gz", "xy"), 0, 0, tiled=True, axis_index_groups=chips)
-    low = shift(mid, "gz", 2)
-    high = shift(mid[..., :7, :], "gz", -2)
-    return compute(low, mid, high, in_weight, env_weight, up_weight, out_weight.reshape(1, -1))
+    far = swap(mid, depth, 2)
+    near = swap(mid[..., :7, :], depth, 0)
+    return compute(far, mid, near, in_weight, env_weight, up_weight, out_weight.reshape(1, -1))
 
 
 def solution(mesh):

time: 61.7 us -> 60.7 us (0.984)
  Pallas kernels: 22.2 us -> 20.1 us
  waiting for transfers between devices: 3.07 us -> 4.22 us
    pallas_call x1, Pallas kernels: 20.7 us -> 18.6 us  [compute(): pl.pallas_call(kernel, out_shape=(jax.ShapeDtypeStruct((2, 2, 128), F32),...]
    ppermute x2, waiting for transfers between devices: 3.07 us -> 4.22 us  [swap(): lax.ppermute(value, 'gz', [(i, ((i + first ^ 2) - first) % count) for i i...]
  transfers between devices with their start and end apart: 2 -> 2, of which waited for: 2 -> 1; matrix products, arithmetic and copies ran while one was open for 0% -> 0% of each run, Pallas kernels for 0% -> 0%
where the time goes in v3:
time: 60.7 us; the launch traced here: 60.3 us
  blocking collectives  20.5 us (34%)
  Pallas kernels  20.1 us (33%)
  starting transfers between devices  14.8 us (24%)
  waiting for transfers between devices  4.22 us (7%)
  between operations  0.68 us (1%)
    all_to_all x1, blocking collectives, body(): lax.all_to_all(packed, ('gz', 'xy'), 0, 0, tiled=True, axis_index_groups=...  20.5 us
    pallas_call x1, Pallas kernels, compute(): pl.pallas_call(kernel, out_shape=(jax.ShapeDtypeStruct((2, 2, 128), F32),...  18.6 us
    ppermute x2, starting transfers between devices, swap(): lax.ppermute(value, 'gz', [(i, ((i + first ^ 2) - first) % count) for i i...  14.8 us
    ppermute x2, waiting for transfers between devices, swap(): lax.ppermute(value, 'gz', [(i, ((i + first ^ 2) - first) % count) for i i...  4.22 us
    pallas_call x1, Pallas kernels, pack(): pl.pallas_call(pack_kernel, out_shape=jax.ShapeDtypeStruct((8, 2, 2, 8, 1...  1.49 us
  transfers between devices with their start and end apart: 2, of which 1 were waited for; matrix products, arithmetic and copies ran while one was open for 0% of the time, Pallas kernels for 0%

profile of v3, /device:TPU:1, one launch (start us, length us, event | category | flops | bytes accessed | tf_op | source)
XLA Modules:
  0.0 60.3 jit_solution(738613153895114569)
XLA Ops:
  0.6 1.5 %pack.1 = f32[8,2,2,8,128]{4,3,2,1,0:T(8,128)} custom-call(f32[3,2,2,128]{3,2,1,0:T(2,128)} %coords_ref.1, s32[2,2,128]{2,1,0:T(2,128)} %species_ref.1, s32[2,2,128]{2,1,0:T(2,128)} %centers_ref.1, s32[2,2,128]{2,1,0:T(2,128)} %others_ref.1, s32[2,2]{1,0:T(2,128)} %live_ref.1), custom_call_target="tpu_custom_call" | custom-call | tf_op jit(solution)/shard_map/pack/pallas_call | solution.py:491
  2.1 0.0 copy-start.3
  2.1 0.0 copy-start.1
  2.1 20.5 %all_to_all.5.mid_ref = f32[8,2,2,8,128]{4,3,2,1,0:T(8,128)S(1)} all-to-all(f32[8,2,2,8,128]{4,3,2,1,0:T(8,128)} %pack.1), channel_id=1, replica_groups={{0,1,2,3,4,5,6,7},{8,9,10,11,12,13,14,15},{16,17,18,19,20,21,22,23},{24..., dimensions={0} | all-to-all | bytes 262144 | tf_op jit(solution)/shard_map/all_to_all | solution.py:513
  22.6 0.0 copy-start
  22.6 12.9 %collective-permute-start = (f32[8,2,2,8,128]{4,3,2,1,0:T(8,128)S(1)}, f32[8,2,2,8,128]{4,3,2,1,0:T(8,128)S(1)}, u32[]{:S(2)}, u32[]{:S(2)}) collective-permute-start(f32[8,2,2,8,128]{4,3,2,1,0:T(8,128)S(1)} %all_to_all.5.mid_ref), channel_id=1, source_target_pairs={{0,760},{4,764},{8,16},{12,20},{16,8},{20,12},{24,32},{28,36},{32,... | collective-permute-start | bytes 393224 | tf_op jit(solution)/shard_map/ppermute | solution.py:501
  35.5 1.9 %collective-permute-start.1 = (f32[8,2,2,7,128]{4,3,2,1,0:T(8,128)S(1)}, f32[8,2,2,7,128]{4,3,2,1,0:T(8,128)S(1)}, u32[]{:S(2)}, u32[]{:S(2)}) collective-permute-start(f32[8,2,2,7,128]{4,3,2,1,0:T(8,128)S(1)} %bitcast.2), channel_id=1, source_target_pairs={{0,8},{4,12},{8,0},{12,4},{16,24},{20,28},{24,16},{28,20},{32,40},... | collective-permute-start | bytes 344072 | tf_op jit(solution)/shard_map/ppermute | solution.py:501
  37.4 0.0 copy-done.3
  37.4 0.1 copy.11.env_ref
  37.5 0.0 copy-start.2
  37.5 4.2 %collective-permute-done.1.near_ref = f32[8,2,2,7,128]{4,3,2,1,0:T(8,128)S(1)} collective-permute-done((f32[8,2,2,7,128]{4,3,2,1,0:T(8,128)S(1)}, f32[8,2,2,7,128]{4,3,2,1,0:T(8,128)S(1)}, u32[]{:S(2)}, u32[]{:S(2)}) %collective-permute-start.1) | collective-permute-done | bytes 114720 | tf_op jit(solution)/shard_map/ppermute | solution.py:501
  41.7 0.0 collective-permute-done.far_ref
  41.7 0.0 copy-done.1
  41.7 0.0 copy-done
  41.7 0.0 copy-done.2
  41.8 18.6 %potential.1 = (f32[2,2,128]{2,1,0:T(2,128)}, f32[3,2,2,128]{3,2,1,0:T(2,128)}) custom-call(f32[8,2,2,8,128]{4,3,2,1,0:T(8,128)S(1)} %collective-permute-done.far_ref, f32[8,2,2,8,128]{4,3,2,1,0:T(8,128)S(1)} %all_to_all.5.mid_ref, f32[8,2,2,7,128]{4,3,2,1,0:T(8,128)S(1)} %collective-permute-done.1.near_ref, f32[24,128]{1,0:T(8,128)S(1)} %copy-done.1, ...), custom_call_target="tpu_custom_call" | custom-call | tf_op jit(solution)/shard_map/potential/pallas_call | solution.py:434
Async XLA Ops:
  2.1 35.3 %copy-start.3 = (f32[128,32]{0,1:T(8,128)S(1)}, f32[128,32]{0,1:T(8,128)}, u32[]{:S(2)}) copy-start(f32[128,32]{0,1:T(8,128)} %param.15) | copy-start | bytes 49156
  2.1 39.6 %copy-start.1 = (f32[24,128]{1,0:T(8,128)S(1)}, f32[24,128]{1,0:T(8,128)}, u32[]{:S(2)}) copy-start(f32[24,128]{1,0:T(8,128)} %in_ref.1) | copy-start | bytes 36868
  22.6 19.1 %copy-start = (f32[160,128]{1,0:T(8,128)S(1)}, f32[160,128]{1,0:T(8,128)}, u32[]{:S(2)}) copy-start(f32[160,128]{1,0:T(8,128)} %up_ref.1) | copy-start | bytes 245764
  22.6 19.1 %collective-permute-start = (f32[8,2,2,8,128]{4,3,2,1,0:T(8,128)S(1)}, f32[8,2,2,8,128]{4,3,2,1,0:T(8,128)S(1)}, u32[]{:S(2)}, u32[]{:S(2)}) collective-permute-start(f32[8,2,2,8,128]{4,3,2,1,0:T(8,128)S(1)} %all_to_all.5.mid_ref), channel_id=1, source_target_pairs={{0,760},{4,764},{8,16},{12,20},{16,8},{20,12},{24,32},{28,36},{32,... | collective-permute-start | bytes 393224 | tf_op jit(solution)/shard_map/ppermute | solution.py:501
  35.5 6.3 %collective-permute-start.1 = (f32[8,2,2,7,128]{4,3,2,1,0:T(8,128)S(1)}, f32[8,2,2,7,128]{4,3,2,1,0:T(8,128)S(1)}, u32[]{:S(2)}, u32[]{:S(2)}) collective-permute-start(f32[8,2,2,7,128]{4,3,2,1,0:T(8,128)S(1)} %bitcast.2), channel_id=1, source_target_pairs={{0,8},{4,12},{8,0},{12,4},{16,24},{20,28},{24,16},{28,20},{32,40},... | collective-permute-start | bytes 344072 | tf_op jit(solution)/shard_map/ppermute | solution.py:501
  37.5 4.2 %copy-start.2 = (f32[128]{0:T(128)S(1)}, f32[128]{0:T(128)}, u32[]{:S(2)}) copy-start(f32[128]{0:T(128)} %param.17) | copy-start | bytes 1540

commit v4 on v3

--- a/solution.py
+++ b/solution.py
@@ -511,8 +511,8 @@
         for chip in range(depth // 2)
     ]
     mid = lax.all_to_all(packed, ("gz", "xy"), 0, 0, tiled=True, axis_index_groups=chips)
-    far = swap(mid, depth, 2)
-    near = swap(mid[..., :7, :], depth, 0)
+    near = swap(mid, depth, 0)
+    far = swap(mid[..., :7, :], depth, 2)
     return compute(far, mid, near, in_weight, env_weight, up_weight, out_weight.reshape(1, -1))
 
 

time: 60.7 us -> 61.2 us (level)
  no operation moved by 1% of the time
where the time goes in v4:
time: 61.2 us; the launch traced here: 60.9 us
  blocking collectives  20.5 us (33%)
  Pallas kernels  20.1 us (33%)
  starting transfers between devices  15.1 us (25%)
  waiting for transfers between devices  4.49 us (7%)
  between operations  0.68 us (1%)
    all_to_all x1, blocking collectives, body(): lax.all_to_all(packed, ('gz', 'xy'), 0, 0, tiled=True, axis_index_groups=...  20.5 us
    pallas_call x1, Pallas kernels, compute(): pl.pallas_call(kernel, out_shape=(jax.ShapeDtypeStruct((2, 2, 128), F32),...  18.6 us
    ppermute x2, starting transfers between devices, swap(): lax.ppermute(value, 'gz', [(i, ((i + first ^ 2) - first) % count) for i i...  15.1 us
    ppermute x2, waiting for transfers between devices, swap(): lax.ppermute(value, 'gz', [(i, ((i + first ^ 2) - first) % count) for i i...  4.49 us
    pallas_call x1, Pallas kernels, pack(): pl.pallas_call(pack_kernel, out_shape=jax.ShapeDtypeStruct((8, 2, 2, 8, 1...  1.49 us
  transfers between devices with their start and end apart: 2, of which 1 were waited for; matrix products, arithmetic and copies ran while one was open for 0% of the time, Pallas kernels for 0%

profile of v4, /device:TPU:1, one launch (start us, length us, event | category | flops | bytes accessed | tf_op | source)
XLA Modules:
  0.0 60.9 jit_solution(11788829204261505087)
XLA Ops:
  0.6 1.5 %pack.1 = f32[8,2,2,8,128]{4,3,2,1,0:T(8,128)} custom-call(f32[3,2,2,128]{3,2,1,0:T(2,128)} %coords_ref.1, s32[2,2,128]{2,1,0:T(2,128)} %species_ref.1, s32[2,2,128]{2,1,0:T(2,128)} %centers_ref.1, s32[2,2,128]{2,1,0:T(2,128)} %others_ref.1, s32[2,2]{1,0:T(2,128)} %live_ref.1), custom_call_target="tpu_custom_call" | custom-call | tf_op jit(solution)/shard_map/pack/pallas_call | solution.py:491
  2.1 0.0 copy-start.3
  2.1 0.0 copy-start.1
  2.1 20.5 %all_to_all.5.mid_ref = f32[8,2,2,8,128]{4,3,2,1,0:T(8,128)S(1)} all-to-all(f32[8,2,2,8,128]{4,3,2,1,0:T(8,128)} %pack.1), channel_id=1, replica_groups={{0,1,2,3,4,5,6,7},{8,9,10,11,12,13,14,15},{16,17,18,19,20,21,22,23},{24..., dimensions={0} | all-to-all | bytes 262144 | tf_op jit(solution)/shard_map/all_to_all | solution.py:513
  22.6 0.0 copy-start
  22.6 2.0 %collective-permute-start.1 = (f32[8,2,2,8,128]{4,3,2,1,0:T(8,128)S(1)}, f32[8,2,2,8,128]{4,3,2,1,0:T(8,128)S(1)}, u32[]{:S(2)}, u32[]{:S(2)}) collective-permute-start(f32[8,2,2,8,128]{4,3,2,1,0:T(8,128)S(1)} %all_to_all.5.mid_ref), channel_id=1, source_target_pairs={{0,8},{4,12},{8,0},{12,4},{16,24},{20,28},{24,16},{28,20},{32,40},... | collective-permute-start | bytes 393224 | tf_op jit(solution)/shard_map/ppermute | solution.py:501
  24.6 13.0 %collective-permute-start = (f32[8,2,2,7,128]{4,3,2,1,0:T(8,128)S(1)}, f32[8,2,2,7,128]{4,3,2,1,0:T(8,128)S(1)}, u32[]{:S(2)}, u32[]{:S(2)}) collective-permute-start(f32[8,2,2,7,128]{4,3,2,1,0:T(8,128)S(1)} %bitcast.2), channel_id=1, source_target_pairs={{0,760},{4,764},{8,16},{12,20},{16,8},{20,12},{24,32},{28,36},{32,... | collective-permute-start | bytes 344072 | tf_op jit(solution)/shard_map/ppermute | solution.py:501
  37.7 0.0 copy-done.3
  37.7 0.1 copy.11.env_ref
  37.8 0.0 copy-start.2
  37.8 4.5 %collective-permute-done.far_ref = f32[8,2,2,7,128]{4,3,2,1,0:T(8,128)S(1)} collective-permute-done((f32[8,2,2,7,128]{4,3,2,1,0:T(8,128)S(1)}, f32[8,2,2,7,128]{4,3,2,1,0:T(8,128)S(1)}, u32[]{:S(2)}, u32[]{:S(2)}) %collective-permute-start) | collective-permute-done | bytes 114720 | tf_op jit(solution)/shard_map/ppermute | solution.py:501
  42.3 0.0 collective-permute-done.1.near_ref
  42.3 0.0 copy-done.1
  42.3 0.0 copy-done
  42.3 0.0 copy-done.2
  42.3 18.6 %potential.1 = (f32[2,2,128]{2,1,0:T(2,128)}, f32[3,2,2,128]{3,2,1,0:T(2,128)}) custom-call(f32[8,2,2,7,128]{4,3,2,1,0:T(8,128)S(1)} %collective-permute-done.far_ref, f32[8,2,2,8,128]{4,3,2,1,0:T(8,128)S(1)} %all_to_all.5.mid_ref, f32[8,2,2,8,128]{4,3,2,1,0:T(8,128)S(1)} %collective-permute-done.1.near_ref, f32[24,128]{1,0:T(8,128)S(1)} %copy-done.1, ...), custom_call_target="tpu_custom_call" | custom-call | tf_op jit(solution)/shard_map/potential/pallas_call | solution.py:434
Async XLA Ops:
  2.1 35.6 %copy-start.3 = (f32[128,32]{0,1:T(8,128)S(1)}, f32[128,32]{0,1:T(8,128)}, u32[]{:S(2)}) copy-start(f32[128,32]{0,1:T(8,128)} %param.15) | copy-start | bytes 49156
  2.1 40.2 %copy-start.1 = (f32[24,128]{1,0:T(8,128)S(1)}, f32[24,128]{1,0:T(8,128)}, u32[]{:S(2)}) copy-start(f32[24,128]{1,0:T(8,128)} %in_ref.1) | copy-start | bytes 36868
  22.6 19.7 %copy-start = (f32[160,128]{1,0:T(8,128)S(1)}, f32[160,128]{1,0:T(8,128)}, u32[]{:S(2)}) copy-start(f32[160,128]{1,0:T(8,128)} %up_ref.1) | copy-start | bytes 245764
  22.6 19.7 %collective-permute-start.1 = (f32[8,2,2,8,128]{4,3,2,1,0:T(8,128)S(1)}, f32[8,2,2,8,128]{4,3,2,1,0:T(8,128)S(1)}, u32[]{:S(2)}, u32[]{:S(2)}) collective-permute-start(f32[8,2,2,8,128]{4,3,2,1,0:T(8,128)S(1)} %all_to_all.5.mid_ref), channel_id=1, source_target_pairs={{0,8},{4,12},{8,0},{12,4},{16,24},{20,28},{24,16},{28,20},{32,40},... | collective-permute-start | bytes 393224 | tf_op jit(solution)/shard_map/ppermute | solution.py:501
  24.6 17.6 %collective-permute-start = (f32[8,2,2,7,128]{4,3,2,1,0:T(8,128)S(1)}, f32[8,2,2,7,128]{4,3,2,1,0:T(8,128)S(1)}, u32[]{:S(2)}, u32[]{:S(2)}) collective-permute-start(f32[8,2,2,7,128]{4,3,2,1,0:T(8,128)S(1)} %bitcast.2), channel_id=1, source_target_pairs={{0,760},{4,764},{8,16},{12,20},{16,8},{20,12},{24,32},{28,36},{32,... | collective-permute-start | bytes 344072 | tf_op jit(solution)/shard_map/ppermute | solution.py:501
  37.8 4.5 %copy-start.2 = (f32[128]{0:T(128)S(1)}, f32[128]{0:T(128)}, u32[]{:S(2)}) copy-start(f32[128]{0:T(128)} %param.17) | copy-start | bytes 1540

commit v5 on v2

--- a/solution.py
+++ b/solution.py
@@ -259,7 +259,8 @@
             feature_group(f, group)
         return carry
 
-    lax.fori_loop(0, 6, feature_step, 0)
+    for f in range(6):
+        feature_step(f, 0)
 
     def energy_group(f, cols, reach, inside_row):
         feat_i, feat_j, weight, hots = [], [], [], []
@@ -334,7 +335,8 @@
         return carry
 
     energy_ref[...] = jnp.zeros_like(energy_ref)
-    lax.fori_loop(1, 5, energy_step, 0)
+    for f in range(1, 5):
+        energy_step(f, 0)
     lax.fori_loop(0, 2, rim_step, 0)
 
     def backward_group(f, cols):
@@ -369,7 +371,8 @@
         return carry
 
     back_s[...] = jnp.zeros_like(back_s)
-    lax.fori_loop(1, 5, backward_step, 0)
+    for f in range(1, 5):
+        backward_step(f, 0)
 
     for f in range(1, 5):
         def got(which):
@@ -421,7 +424,7 @@
 
 
 FEATURE_GROUPS = ((0, 1, 2, 3, 4, 5),)
-ENERGY_GROUPS = ((1, 2, 3, 4), (0, 5))
+ENERGY_GROUPS = ((0, 5), (1, 2, 3, 4))
 RIM_GROUPS = ((0, 1, 2, 3, 4, 5),)
 BACK_GROUPS = ((1, 2, 3, 4),)
 

time: 61.7 us -> 59.5 us (0.964)
  Pallas kernels: 22.2 us -> 20 us
    pallas_call x1, Pallas kernels: 20.7 us -> 18.5 us  [compute(): pl.pallas_call(kernel, out_shape=(jax.ShapeDtypeStruct((2, 2, 128), F32),...]
where the time goes in v5:
time: 59.5 us; the launch traced here: 59.2 us
  blocking collectives  20.5 us (34%)
  Pallas kernels  20 us (34%)
  starting transfers between devices  14.8 us (25%)
  waiting for transfers between devices  3.07 us (5%)
  between operations  0.67 us (1%)
    all_to_all x1, blocking collectives, body(): lax.all_to_all(packed, ('gz', 'xy'), 0, 0, tiled=True, axis_index_groups=...  20.5 us
    pallas_call x1, Pallas kernels, compute(): pl.pallas_call(kernel, out_shape=(jax.ShapeDtypeStruct((2, 2, 128), F32),...  18.5 us
    ppermute x2, starting transfers between devices, shift(): lax.ppermute(value, axis, [(i, (i + step) % count) for i in range(count)])  14.8 us
    ppermute x2, waiting for transfers between devices, shift(): lax.ppermute(value, axis, [(i, (i + step) % count) for i in range(count)])  3.07 us
    pallas_call x1, Pallas kernels, pack(): pl.pallas_call(pack_kernel, out_shape=jax.ShapeDtypeStruct((8, 2, 2, 8, 1...  1.49 us
  transfers between devices with their start and end apart: 2, of which 2 were waited for; matrix products, arithmetic and copies ran while one was open for 0% of the time, Pallas kernels for 0%

profile of v5, /device:TPU:1, one launch (start us, length us, event | category | flops | bytes accessed | tf_op | source)
XLA Modules:
  0.0 59.2 jit_solution(7948663899212235889)
XLA Ops:
  0.6 1.5 %pack.1 = f32[8,2,2,8,128]{4,3,2,1,0:T(8,128)} custom-call(f32[3,2,2,128]{3,2,1,0:T(2,128)} %coords_ref.1, s32[2,2,128]{2,1,0:T(2,128)} %species_ref.1, s32[2,2,128]{2,1,0:T(2,128)} %centers_ref.1, s32[2,2,128]{2,1,0:T(2,128)} %others_ref.1, s32[2,2]{1,0:T(2,128)} %live_ref.1), custom_call_target="tpu_custom_call" | custom-call | tf_op jit(solution)/shard_map/pack/pallas_call | solution.py:490
  2.1 0.0 copy-start.3
  2.1 0.0 copy-start.1
  2.1 20.5 %all_to_all.5.mid_ref = f32[8,2,2,8,128]{4,3,2,1,0:T(8,128)S(1)} all-to-all(f32[8,2,2,8,128]{4,3,2,1,0:T(8,128)} %pack.1), channel_id=1, replica_groups={{0,1,2,3,4,5,6,7},{8,9,10,11,12,13,14,15},{16,17,18,19,20,21,22,23},{24..., dimensions={0} | all-to-all | bytes 262144 | tf_op jit(solution)/shard_map/all_to_all | solution.py:513
  22.6 0.0 copy-start
  22.6 2.0 %collective-permute-start = (f32[8,2,2,8,128]{4,3,2,1,0:T(8,128)S(1)}, f32[8,2,2,8,128]{4,3,2,1,0:T(8,128)S(1)}, u32[]{:S(2)}, u32[]{:S(2)}) collective-permute-start(f32[8,2,2,8,128]{4,3,2,1,0:T(8,128)S(1)} %all_to_all.5.mid_ref), channel_id=1, source_target_pairs={{0,8},{4,12},{8,16},{12,20},{16,24},{20,28},{24,32},{28,36},{32,40... | collective-permute-start | bytes 393224 | tf_op jit(solution)/shard_map/ppermute | solution.py:501
  24.6 12.8 %collective-permute-start.1 = (f32[8,2,2,7,128]{4,3,2,1,0:T(8,128)S(1)}, f32[8,2,2,7,128]{4,3,2,1,0:T(8,128)S(1)}, u32[]{:S(2)}, u32[]{:S(2)}) collective-permute-start(f32[8,2,2,7,128]{4,3,2,1,0:T(8,128)S(1)} %bitcast.2), channel_id=1, source_target_pairs={{0,760},{4,764},{8,0},{12,4},{16,8},{20,12},{24,16},{28,20},{32,24... | collective-permute-start | bytes 344072 | tf_op jit(solution)/shard_map/ppermute | solution.py:501
  37.4 0.0 copy-done.3
  37.4 0.1 copy.11.env_ref
  37.5 0.0 copy-start.2
  37.5 2.3 %collective-permute-done.1.high_ref = f32[8,2,2,7,128]{4,3,2,1,0:T(8,128)S(1)} collective-permute-done((f32[8,2,2,7,128]{4,3,2,1,0:T(8,128)S(1)}, f32[8,2,2,7,128]{4,3,2,1,0:T(8,128)S(1)}, u32[]{:S(2)}, u32[]{:S(2)}) %collective-permute-start.1) | collective-permute-done | bytes 114720 | tf_op jit(solution)/shard_map/ppermute | solution.py:501
  39.9 0.7 %collective-permute-done.low_ref = f32[8,2,2,8,128]{4,3,2,1,0:T(8,128)S(1)} collective-permute-done((f32[8,2,2,8,128]{4,3,2,1,0:T(8,128)S(1)}, f32[8,2,2,8,128]{4,3,2,1,0:T(8,128)S(1)}, u32[]{:S(2)}, u32[]{:S(2)}) %collective-permute-start) | collective-permute-done | bytes 131104 | tf_op jit(solution)/shard_map/ppermute | solution.py:501
  40.6 0.0 copy-done.1
  40.6 0.0 copy-done
  40.6 0.0 copy-done.2
  40.6 18.5 %potential.1 = (f32[2,2,128]{2,1,0:T(2,128)}, f32[3,2,2,128]{3,2,1,0:T(2,128)}) custom-call(f32[8,2,2,8,128]{4,3,2,1,0:T(8,128)S(1)} %collective-permute-done.low_ref, f32[8,2,2,8,128]{4,3,2,1,0:T(8,128)S(1)} %all_to_all.5.mid_ref, f32[8,2,2,7,128]{4,3,2,1,0:T(8,128)S(1)} %collective-permute-done.1.high_ref, f32[24,128]{1,0:T(8,128)S(1)} %copy-done.1, ...), custom_call_target="tpu_custom_call" | custom-call | tf_op jit(solution)/shard_map/potential/pallas_call | solution.py:433
Async XLA Ops:
  2.1 35.3 %copy-start.3 = (f32[128,32]{0,1:T(8,128)S(1)}, f32[128,32]{0,1:T(8,128)}, u32[]{:S(2)}) copy-start(f32[128,32]{0,1:T(8,128)} %param.15) | copy-start | bytes 49156
  2.1 38.5 %copy-start.1 = (f32[24,128]{1,0:T(8,128)S(1)}, f32[24,128]{1,0:T(8,128)}, u32[]{:S(2)}) copy-start(f32[24,128]{1,0:T(8,128)} %in_ref.1) | copy-start | bytes 36868
  22.6 18.0 %copy-start = (f32[160,128]{1,0:T(8,128)S(1)}, f32[160,128]{1,0:T(8,128)}, u32[]{:S(2)}) copy-start(f32[160,128]{1,0:T(8,128)} %up_ref.1) | copy-start | bytes 245764
  22.6 18.0 %collective-permute-start = (f32[8,2,2,8,128]{4,3,2,1,0:T(8,128)S(1)}, f32[8,2,2,8,128]{4,3,2,1,0:T(8,128)S(1)}, u32[]{:S(2)}, u32[]{:S(2)}) collective-permute-start(f32[8,2,2,8,128]{4,3,2,1,0:T(8,128)S(1)} %all_to_all.5.mid_ref), channel_id=1, source_target_pairs={{0,8},{4,12},{8,16},{12,20},{16,24},{20,28},{24,32},{28,36},{32,40... | collective-permute-start | bytes 393224 | tf_op jit(solution)/shard_map/ppermute | solution.py:501
  24.6 15.2 %collective-permute-start.1 = (f32[8,2,2,7,128]{4,3,2,1,0:T(8,128)S(1)}, f32[8,2,2,7,128]{4,3,2,1,0:T(8,128)S(1)}, u32[]{:S(2)}, u32[]{:S(2)}) collective-permute-start(f32[8,2,2,7,128]{4,3,2,1,0:T(8,128)S(1)} %bitcast.2), channel_id=1, source_target_pairs={{0,760},{4,764},{8,0},{12,4},{16,8},{20,12},{24,16},{28,20},{32,24... | collective-permute-start | bytes 344072 | tf_op jit(solution)/shard_map/ppermute | solution.py:501
  37.5 3.1 %copy-start.2 = (f32[128]{0:T(128)S(1)}, f32[128]{0:T(128)}, u32[]{:S(2)}) copy-start(f32[128]{0:T(128)} %param.17) | copy-start | bytes 1540
